TPU v7x, 256 devices: a whole 4x4x8 slice. The times are simulated.
256 devices in a mesh: gx: 4 (over z_hi), gy: 8 (over z_lo, x), gz: 8 (over y, core).
Axes of the slice: x: 4, y: 4, z: 8 (z_hi: 4, z_lo: 2; z = z_hi * 2 + z_lo), core: 2. Of those that a mesh axis runs over, the one named last changes fastest.
Arguments:
- spectrum_real: float32 [512, 512, 512], P(None, ('gx', 'gy', 'gz')), may hold values from -6 to 6
- spectrum_imag: float32 [512, 512, 512], P(None, ('gx', 'gy', 'gz')), may hold values from -6 to 6
- volume: float32 [512, 512, 512], P('gy', 'gz', 'gx'), may hold values from -6 to 6
- weights: float32 [512, 512, 512], P('gy', 'gz', 'gx'), may hold values from 0.3 to 3
Outputs:
- updated: float32 [512, 512, 512], P('gy', 'gz', 'gx')
All inputs are finite; a program needn't handle non-finite values.
Results may differ from a plain program's by a relative error of at most 0.000075.
Values sent between devices are 32-bit elements; how exact they have to be, the bound alone decides.
A program may use at most 128 MiB of HBM per device.

v0:
```python
import math

import jax
import jax.numpy as jnp
from jax import lax
from jax.sharding import PartitionSpec as P

NY = 512
NZ = 512
NX = 512


step_size = 0.5
tv_weight = 0.5
smoothing = 0.5
highest = lax.Precision.HIGHEST


def padded_2(x, sides, width):
    for axis, dim in sides:
        size, length = (lax.axis_size(axis), x.shape[dim])
        up = [(i, (i + 1) % size) for i in range(size - 1)]
        down = [(j, i) for i, j in up]
        last = lax.slice_in_dim(x, length - width, length, axis=dim)
        initial = lax.slice_in_dim(x, 0, width, axis=dim)
        before = lax.ppermute(last, axis, up)
        after = lax.ppermute(initial, axis, down)
        x = jnp.concatenate([before, x, after], axis=dim)
    return x


def dft_tables(length):
    positions = jnp.arange(length, dtype=jnp.int32)
    phases = positions[:, None] * positions[None, :] % length
    angles = phases.astype(jnp.float32) * (2.0 * math.pi / length)
    factor = 1.0 / math.sqrt(length)
    return (jnp.cos(angles) * factor, jnp.sin(angles) * factor)


def depth_transform(pieces):
    real_in, imag_in = pieces
    cos_depth, sin_depth = dft_tables(real_in.shape[1])
    first = jnp.einsum(
        "nk,ykx->ynx", cos_depth, real_in, precision=highest, preferred_element_type=jnp.float32
    )
    second = jnp.einsum(
        "nk,ykx->ynx", sin_depth, imag_in, precision=highest, preferred_element_type=jnp.float32
    )
    return first - second


def width_transform(real_part, imag_part):
    shape_now = real_part.shape
    width = shape_now[2]
    cos_cols, sin_cols = dft_tables(width)
    flat_real = real_part.reshape(-1, width)
    flat_imag = imag_part.reshape(-1, width)
    real_out = (
        jnp.dot(flat_real, cos_cols, precision=highest)
        - jnp.dot(flat_imag, sin_cols, precision=highest)
    ).reshape(shape_now)
    imag_out = (
        jnp.dot(flat_real, sin_cols, precision=highest)
        + jnp.dot(flat_imag, cos_cols, precision=highest)
    ).reshape(shape_now)
    return (real_out, imag_out)


def region(field, start_y, start_z, start_x, size_y, size_z, size_x):
    return field[start_y : start_y + size_y, start_z : start_z + size_z, start_x : start_x + size_x]


def on_device(spectrum_real, spectrum_imag, volume, weights):
    stacked = jnp.stack([volume, weights])
    padded = padded_2(stacked, (("gx", 3), ("gy", 1), ("gz", 2)), 1)
    brick_y, brick_z, brick_x = volume.shape
    span_y, span_z, span_x = (brick_y + 1, brick_z + 1, brick_x + 1)
    field = padded[0]
    edge_weights = padded[1]
    base = region(field, 0, 0, 0, span_y, span_z, span_x)
    global_y = lax.axis_index("gy") * brick_y + jnp.arange(span_y, dtype=jnp.int32) - 1
    global_z = lax.axis_index("gz") * brick_z + jnp.arange(span_z, dtype=jnp.int32) - 1
    global_x = lax.axis_index("gx") * brick_x + jnp.arange(span_x, dtype=jnp.int32) - 1
    slope_y = region(field, 1, 0, 0, span_y, span_z, span_x) - base
    slope_z = region(field, 0, 1, 0, span_y, span_z, span_x) - base
    slope_x = region(field, 0, 0, 1, span_y, span_z, span_x) - base
    slope_y = jnp.where((global_y < NY - 1)[:, None, None], slope_y, 0.0)
    slope_z = jnp.where((global_z < NZ - 1)[None, :, None], slope_z, 0.0)
    slope_x = jnp.where((global_x < NX - 1)[None, None, :], slope_x, 0.0)
    magnitude = jnp.sqrt(slope_y * slope_y + slope_z * slope_z + slope_x * slope_x + smoothing)
    inside = (
        (global_y >= 0)[:, None, None]
        & (global_z >= 0)[None, :, None]
        & (global_x >= 0)[None, None, :]
    )
    scaled = jnp.where(
        inside, region(edge_weights, 0, 0, 0, span_y, span_z, span_x) / magnitude, 0.0
    )
    flux_y = scaled * slope_y
    flux_z = scaled * slope_z
    flux_x = scaled * slope_x
    tv_grad = flux_y[:-1, 1:, 1:] - flux_y[1:, 1:, 1:]
    tv_grad = tv_grad + flux_z[1:, :-1, 1:] - flux_z[1:, 1:, 1:]
    tv_grad = tv_grad + flux_x[1:, 1:, :-1] - flux_x[1:, 1:, 1:]
    rows = spectrum_real.shape[0]
    cos_rows, sin_rows = dft_tables(rows)
    flat_real = spectrum_real.reshape(rows, -1)
    flat_imag = spectrum_imag.reshape(rows, -1)
    real_part = (
        jnp.dot(cos_rows, flat_real, precision=highest)
        - jnp.dot(sin_rows, flat_imag, precision=highest)
    ).reshape(spectrum_real.shape)
    imag_part = (
        jnp.dot(sin_rows, flat_real, precision=highest)
        + jnp.dot(cos_rows, flat_imag, precision=highest)
    ).reshape(spectrum_real.shape)
    real_part, imag_part = (
        lax.all_to_all(real_part, ("gy", "gz"), split_axis=0, concat_axis=1, tiled=True),
        lax.all_to_all(imag_part, ("gy", "gz"), split_axis=0, concat_axis=1, tiled=True),
    )
    real_part, imag_part = width_transform(real_part, imag_part)
    projected = depth_transform(
        (
            lax.all_to_all(real_part, "gx", split_axis=2, concat_axis=1, tiled=True),
            lax.all_to_all(imag_part, "gx", split_axis=2, concat_axis=1, tiled=True),
        )
    )
    data_term = lax.all_to_all(projected, "gz", split_axis=1, concat_axis=0, tiled=True)
    return volume - step_size * (data_term + tv_weight * tv_grad)


def solution(mesh):
    in_specs = (
        P(None, ("gx", "gy", "gz"), None),
        P(None, ("gx", "gy", "gz"), None),
        P("gy", "gz", "gx"),
        P("gy", "gz", "gx"),
    )
    out_specs = P("gy", "gz", "gx")
    return jax.shard_map(
        on_device, mesh=mesh, in_specs=in_specs, out_specs=out_specs, check_vma=False
    )
```

profile of v0, /device:TPU:1, one launch (start us, length us, event | category | flops | bytes accessed | tf_op | source)
XLA Modules:
  0.0 356.9 jit_solution(9612182292552647373)
XLA Ops:
  0.0 2.1 copy.35
  2.1 7.4 %fusion.19 = f32[512,1024]{1,0:T(8,128)S(1)} fusion(f32[512,1024]{1,0:T(8,128)S(1)} %bitcast.73), kind=kOutput, calls=%fused_computation.47 | convolution fusion | flops 3225157632 | bytes 4194304 | tf_op jit(solution)/shard_map/dot_general | solution.py:110
  11.3 7.7 %convolution_subtract_fusion.1 = f32[512,1024]{1,0:T(8,128)S(1)} fusion(f32[512,1024]{1,0:T(8,128)S(1)} %fusion.19, f32[512,1024]{1,0:T(8,128)S(1)} %bitcast.75), kind=kOutput, calls=%fused_computation.30 | convolution fusion | flops 3225681920 | bytes 6291456 | tf_op jit(solution)/shard_map/dot_general | solution.py:111
  19.0 2.8 reshape.87
  21.8 10.3 %all-to-all-start = ((f32[512,2,512]{2,1,0:T(2,128)}), f32[512,2,512]{2,1,0:T(2,128)S(1)}, u32[]{:S(2)}, u32[]{:S(2)}) async-start(f32[512,2,512]{2,1,0:T(2,128)} %reshape.87), calls=%async_computation | async-start | bytes 4194304 | tf_op jit(solution)/shard_map/all_to_all | solution.py:118
  32.1 9.1 %fusion.21 = f32[512,1024]{1,0:T(8,128)S(1)} fusion(f32[512,1024]{1,0:T(8,128)} %bitcast.74), kind=kOutput, calls=%fused_computation.49 | convolution fusion | flops 3225157632 | bytes 4194304 | tf_op jit(solution)/shard_map/dot_general | solution.py:114
  41.3 8.7 %convolution_add_fusion.1 = f32[512,1024]{1,0:T(8,128)} fusion(f32[512,1024]{1,0:T(8,128)S(1)} %fusion.21, f32[512,1024]{1,0:T(8,128)S(1)} %bitcast.76), kind=kOutput, calls=%fused_computation.29 | convolution fusion | flops 3225681920 | bytes 6291456 | tf_op jit(solution)/shard_map/dot_general | solution.py:115
  50.0 4.0 %reshape.89 = f32[512,2,512]{2,1,0:T(2,128)} reshape(f32[512,1024]{1,0:T(8,128)} %convolution_add_fusion.1) | data formatting | bytes 4194304 | tf_op jit(solution)/shard_map/reshape | solution.py:116
  54.0 5.9 %all-to-all-done = f32[512,2,512]{2,1,0:T(2,128)S(1)} async-done(((f32[512,2,512]{2,1,0:T(2,128)}), f32[512,2,512]{2,1,0:T(2,128)S(1)}, u32[]{:S(2)}, u32[]{:S(2)}) %all-to-all-start) | async-done | bytes 2097184 | tf_op jit(solution)/shard_map/all_to_all | solution.py:118
  59.9 17.8 %all-to-all-start.1 = ((f32[512,2,512]{2,1,0:T(2,128)}), f32[512,2,512]{2,1,0:T(2,128)}, u32[]{:S(2)}, u32[]{:S(2)}) async-start(f32[512,2,512]{2,1,0:T(2,128)} %reshape.89), calls=%async_computation.1 | async-start | bytes 4194304 | tf_op jit(solution)/shard_map/all_to_all | solution.py:119
  79.8 2.4 reshape.88
  82.3 10.1 %fusion.18 = f32[1024,512]{1,0:T(8,128)} fusion(f32[1024,512]{1,0:T(8,128)} %reshape.88), kind=kOutput, calls=%fused_computation.46 | convolution fusion | flops 3225157632 | bytes 4194304 | tf_op jit(solution)/shard_map/dot_general | solution.py:59
  92.4 13.2 %all-to-all-done.1 = f32[512,2,512]{2,1,0:T(2,128)} async-done(((f32[512,2,512]{2,1,0:T(2,128)}), f32[512,2,512]{2,1,0:T(2,128)}, u32[]{:S(2)}, u32[]{:S(2)}) %all-to-all-start.1) | async-done | bytes 2097184 | tf_op jit(solution)/shard_map/all_to_all | solution.py:119
  105.5 2.0 copy.43
  107.5 2.9 copy.22
  110.5 2.7 reshape.90
  113.2 10.5 %convolution_subtract_fusion = f32[1024,512]{1,0:T(8,128)} fusion(f32[1024,512]{1,0:T(8,128)} %fusion.18, f32[1024,512]{1,0:T(8,128)S(1)} %reshape.90), kind=kOutput, calls=%fused_computation.28 | convolution fusion | flops 3225681920 | bytes 6291456 | tf_op jit(solution)/shard_map/dot_general | solution.py:60
  123.7 3.0 copy.23
  126.7 7.8 %all-to-all-start.2 = ((f32[8,128,512]{1,0,2:T(8,128)}), f32[8,128,512]{1,0,2:T(8,128)}, u32[]{:S(2)}, u32[]{:S(2)}) async-start(f32[8,128,512]{1,0,2:T(8,128)} %copy.23), calls=%async_computation.2 | async-start | bytes 4194304 | tf_op jit(solution)/shard_map/all_to_all | solution.py:124
  134.5 8.4 %fusion.20 = f32[1024,512]{1,0:T(8,128)S(1)} fusion(f32[1024,512]{1,0:T(8,128)S(1)} %copy-done.5), kind=kOutput, calls=%fused_computation.48 | convolution fusion | flops 3225157632 | bytes 4194304 | tf_op jit(solution)/shard_map/dot_general | solution.py:63
  143.0 8.4 %convolution_add_fusion = f32[1024,512]{1,0:T(8,128)S(1)} fusion(f32[1024,512]{1,0:T(8,128)S(1)} %fusion.20, f32[1024,512]{1,0:T(8,128)S(1)} %copy-done.7), kind=kOutput, calls=%fused_computation.27 | convolution fusion | flops 3225681920 | bytes 6291456 | tf_op jit(solution)/shard_map/dot_general | solution.py:64
  153.2 13.7 %all-to-all-done.2 = f32[8,128,512]{1,0,2:T(8,128)} async-done(((f32[8,128,512]{1,0,2:T(8,128)}), f32[8,128,512]{1,0,2:T(8,128)}, u32[]{:S(2)}, u32[]{:S(2)}) %all-to-all-start.2) | async-done | bytes 2097184 | tf_op jit(solution)/shard_map/all_to_all | solution.py:124
  166.9 18.2 %all-to-all-start.3 = ((f32[8,128,512]{1,0,2:T(8,128)}), f32[8,128,512]{1,0,2:T(8,128)}, u32[]{:S(2)}, u32[]{:S(2)}) async-start(f32[8,128,512]{1,0,2:T(8,128)} %copy.25), calls=%async_computation.3 | async-start | bytes 4194304 | tf_op jit(solution)/shard_map/all_to_all | solution.py:125
  185.1 6.5 %slice_maximum_fusion = (f32[2,64,64,1]{3,2,1,0:T(8,128)}, f32[2,64,64,1]{3,2,1,0:T(8,128)}) fusion(f32[1,64,64,128]{3,2,1,0:T(8,128)} %bitcast.63, f32[1,64,64,128]{3,2,1,0:T(8,128)S(1)} %bitcast.59), kind=kLoop, calls=%fused_computation.12 | loop fusion | flops 16384 | bytes 4259840 | tf_op jit(solution)/shard_map/stack | solution.py:74
  191.6 3.0 copy.30
  194.6 4.3 %collective-permute-start = (f32[2,64,64,1]{2,1,3,0:T(8,128)S(1)}, f32[2,64,64,1]{2,1,3,0:T(8,128)S(1)}, u32[]{:S(2)}, u32[]{:S(2)}) collective-permute-start(f32[2,64,64,1]{2,1,3,0:T(8,128)S(1)} %copy.30), channel_id=1, source_target_pairs={{0,64},{64,128},{128,192},{1,65},{65,129},{129,193},{2,66},{66,130... | collective-permute-start | bytes 98312 | tf_op jit(solution)/shard_map/ppermute | solution.py:26
  198.8 3.0 copy.31
  203.2 8.3 %collective-permute-done = f32[2,64,64,1]{2,1,3,0:T(8,128)S(1)} collective-permute-done((f32[2,64,64,1]{2,1,3,0:T(8,128)S(1)}, f32[2,64,64,1]{2,1,3,0:T(8,128)S(1)}, u32[]{:S(2)}, u32[]{:S(2)}) %collective-permute-start) | collective-permute-done | bytes 32800 | tf_op jit(solution)/shard_map/ppermute | solution.py:26
  211.5 2.8 copy.32
  214.3 25.2 %collective-permute-done.1 = f32[2,64,64,1]{2,1,3,0:T(8,128)S(1)} collective-permute-done((f32[2,64,64,1]{2,1,3,0:T(8,128)S(1)}, f32[2,64,64,1]{2,1,3,0:T(8,128)S(1)}, u32[]{:S(2)}, u32[]{:S(2)}) %collective-permute-start.1) | collective-permute-done | bytes 32800 | tf_op jit(solution)/shard_map/ppermute | solution.py:27
  239.5 2.7 copy.33
  247.8 6.8 %collective-permute-done.3 = f32[2,1,64,130]{3,2,1,0:T(8,128)S(1)} collective-permute-done((f32[2,1,64,130]{3,2,1,0:T(8,128)S(1)}, f32[2,1,64,130]{3,2,1,0:T(8,128)S(1)}, u32[]{:S(2)}, u32[]{:S(2)}) %collective-permute-start.3) | collective-permute-done | bytes 66592 | tf_op jit(solution)/shard_map/ppermute | solution.py:27
  255.5 2.6 collective-permute-start.4
  260.0 4.3 %collective-permute-done.5 = f32[2,66,1,130]{3,2,1,0:T(1,128)S(1)} collective-permute-done((f32[2,66,1,130]{3,2,1,0:T(1,128)S(1)}, f32[2,66,1,130]{3,2,1,0:T(1,128)S(1)}, u32[]{:S(2)}, u32[]{:S(2)}) %collective-permute-start.5) | collective-permute-done | bytes 68672 | tf_op jit(solution)/shard_map/ppermute | solution.py:27
  264.4 7.3 %pad_maximum_fusion = f32[2,66,66,130]{3,2,1,0:T(8,128)S(1)} fusion(f32[2,66,1,130]{3,2,1,0:T(1,128)S(1)} %collective-permute-done.5, f32[2,1,64,130]{3,2,1,0:T(8,128)S(1)} %collective-permute-done.3, f32[2,64,64,1]{3,2,1,0:T(8,128)S(1)} %copy-done.1, f32[1,64,64,128]{3,2,1,0:T(8,128)S(1)} %bitcast.66, f32[1,64,64,128]{3,2,1,0:T(8,128)S(1)} %bitcast.62, ...), kind=kLoop, calls=%fused_computation | loop fusion | flops 7927920 | bytes 9060480 | tf_op jit(solution)/shard_map/concatenate | solution.py:28
  271.7 4.4 %slice_bitcast_fusion.1 = (f32[66,66,130]{2,1,0:T(8,128)}, f32[66,66,130]{2,1,0:T(8,128)}) fusion(f32[2,66,66,130]{3,2,1,0:T(8,128)S(1)} %pad_maximum_fusion), kind=kLoop, calls=%fused_computation.2 | loop fusion | bytes 9060480 | tf_op jit(solution)/shard_map/squeeze | solution.py:79
  276.0 4.3 %copy.42 = f32[8,128,4,128]{1,2,3,0:T(4,128)} copy(f32[8,128,4,128]{1,0,3,2:T(8,128)} %bitcast.5) | data formatting | bytes 4194304 | tf_op jit(solution)/shard_map/all_to_all | solution.py:124
  280.3 3.1 all_to_all.70
  283.4 9.9 %fusion.13 = f32[8,128,512]{2,1,0:T(8,128)} fusion(f32[8,512,128]{1,2,0:T(8,128)} %all_to_all.70), kind=kOutput, calls=%fused_computation.39 | convolution fusion | flops 3225157632 | bytes 4194304 | tf_op jit(solution)/shard_map/nk,ykx->ynx/dot_general | solution.py:43
  293.3 4.3 %copy.41 = f32[8,128,4,128]{1,2,3,0:T(4,128)} copy(f32[8,128,4,128]{1,0,3,2:T(8,128)} %bitcast.9) | data formatting | bytes 4194304 | tf_op jit(solution)/shard_map/all_to_all | solution.py:125
  297.6 3.0 all_to_all.74
  300.7 10.6 %subtract_bitcast_fusion = f32[8,512,128]{1,2,0:T(8,128)} fusion(f32[8,128,512]{2,1,0:T(8,128)} %fusion.13, f32[8,512,128]{1,2,0:T(8,128)} %all_to_all.74), kind=kOutput, calls=%fused_computation.26 | convolution fusion | flops 3225681920 | bytes 6291456 | tf_op jit(solution)/shard_map/nk,ykx->ynx/dot_general | solution.py:46
  311.3 2.9 copy.27
  314.2 4.4 %all-to-all-start.4 = ((f32[8,512,128]{2,0,1:T(8,128)}), f32[8,512,128]{2,0,1:T(8,128)}, u32[]{:S(2)}, u32[]{:S(2)}) async-start(f32[8,512,128]{2,0,1:T(8,128)} %copy.27), calls=%async_computation.4 | async-start | bytes 4194304 | tf_op jit(solution)/shard_map/all_to_all | solution.py:128
  318.6 14.3 %fusion.42 = (f32[65,65,129]{2,1,0:T(8,128)}, f32[65,65,129]{2,1,0:T(8,128)S(1)}) fusion(f32[66,66,130]{2,1,0:T(8,128)} %get-tuple-element.12, pred[65]{0:T(512)(128)(4,1)S(1)} %get-tuple-element.21, pred[129]{0:T(512)(128)(4,1)S(1)} %get-tuple-element.17, pred[65]{0:T(512)(128)(4,1)S(1)} %get-tuple-element.22, f32[66,66,130]{2,1,0:T(8,128)} %get-tuple-element.11, ...), kind=kLoop, calls=%fused_computation.70 | loop fusion | flops 8720400 | bytes 15265313 | tf_op jit(solution)/shard_map/mul | solution.py:99
  332.9 4.7 %fusion.43 = (f32[65,65,129]{2,1,0:T(8,128)}, f32[65,65,129]{2,1,0:T(8,128)}) fusion(f32[65,65,129]{2,1,0:T(8,128)S(1)} %get-tuple-element.6, f32[66,66,130]{2,1,0:T(8,128)S(1)} %bitcast.58, pred[65]{0:T(512)(128)(4,1)S(1)} %get-tuple-element.22, pred[129]{0:T(512)(128)(4,1)S(1)} %get-tuple-element.17), kind=kLoop, calls=%fused_computation.71 | loop fusion | flops 3270150 | bytes 13080794 | tf_op jit(solution)/shard_map/mul | solution.py:100
  337.6 6.0 %all-to-all-done.4 = f32[8,512,128]{2,0,1:T(8,128)} async-done(((f32[8,512,128]{2,0,1:T(8,128)}), f32[8,512,128]{2,0,1:T(8,128)}, u32[]{:S(2)}, u32[]{:S(2)}) %all-to-all-start.4) | async-done | bytes 2097184 | tf_op jit(solution)/shard_map/all_to_all | solution.py:128
  345.5 11.2 %fusion.7 = f32[64,64,128]{2,1,0:T(8,128)} fusion(f32[64,64,128]{2,1,0:T(8,128)S(1)} %copy-done.2, f32[65,65,129]{2,1,0:T(8,128)} %get-tuple-element.14, f32[65,65,129]{2,1,0:T(8,128)} %get-tuple-element.13, f32[65,65,129]{2,1,0:T(8,128)} %get-tuple-element.5, f32[8,8,64,128]{3,2,1,0:T(8,128)S(1)} %copy.29), kind=kLoop, calls=%fused_computation.17 | loop fusion | flops 4718592 | bytes 18874368 | tf_op jit(solution)/shard_map/sub | solution.py:129
  (45 shorter events, 17.4 us)
Async XLA Ops:
  2.1 7.4 %copy-start.8 = (f32[64,8,2,512]{3,1,2,0:T(8,128)}, f32[64,8,2,512]{3,1,2,0:T(8,128)S(1)}, u32[]{:S(2)}) copy-start(f32[64,8,2,512]{3,1,2,0:T(8,128)S(1)} %copy.35) | copy-start | bytes 6291460
  2.1 7.4 %copy-start.4 = (f32[512,2,512]{2,1,0:T(2,128)S(1)}, f32[512,2,512]{2,1,0:T(2,128)}, u32[]{:S(2)}) copy-start(f32[512,2,512]{2,1,0:T(2,128)} %param.5) | copy-start | bytes 6291460
  10.0 1.3 copy-start.9
  21.8 38.2 %all-to-all-start = ((f32[512,2,512]{2,1,0:T(2,128)}), f32[512,2,512]{2,1,0:T(2,128)S(1)}, u32[]{:S(2)}, u32[]{:S(2)}) async-start(f32[512,2,512]{2,1,0:T(2,128)} %reshape.87), calls=%async_computation | async-start | bytes 4194304 | tf_op jit(solution)/shard_map/all_to_all | solution.py:118
  32.1 9.1 %copy-start.10 = (f32[64,8,2,512]{3,1,2,0:T(8,128)S(1)}, f32[64,8,2,512]{3,1,2,0:T(8,128)}, u32[]{:S(2)}) copy-start(f32[64,8,2,512]{3,1,2,0:T(8,128)} %copy-done.9) | copy-start | bytes 6291460
  59.9 45.6 %all-to-all-start.1 = ((f32[512,2,512]{2,1,0:T(2,128)}), f32[512,2,512]{2,1,0:T(2,128)}, u32[]{:S(2)}, u32[]{:S(2)}) async-start(f32[512,2,512]{2,1,0:T(2,128)} %reshape.89), calls=%async_computation.1 | async-start | bytes 4194304 | tf_op jit(solution)/shard_map/all_to_all | solution.py:119
  113.2 10.5 %copy-start.6 = (f32[1024,512]{1,0:T(8,128)}, f32[1024,512]{1,0:T(8,128)S(1)}, u32[]{:S(2)}) copy-start(f32[1024,512]{1,0:T(8,128)S(1)} %reshape.90) | copy-start | bytes 6291460
  126.7 7.8 %copy-start.5 = (f32[1024,512]{1,0:T(8,128)S(1)}, f32[1024,512]{1,0:T(8,128)}, u32[]{:S(2)}) copy-start(f32[1024,512]{1,0:T(8,128)} %reshape.88) | copy-start | bytes 6291460
  126.7 40.2 %all-to-all-start.2 = ((f32[8,128,512]{1,0,2:T(8,128)}), f32[8,128,512]{1,0,2:T(8,128)}, u32[]{:S(2)}, u32[]{:S(2)}) async-start(f32[8,128,512]{1,0,2:T(8,128)} %copy.23), calls=%async_computation.2 | async-start | bytes 4194304 | tf_op jit(solution)/shard_map/all_to_all | solution.py:124
  134.5 8.4 %copy-start.7 = (f32[1024,512]{1,0:T(8,128)S(1)}, f32[1024,512]{1,0:T(8,128)}, u32[]{:S(2)}) copy-start(f32[1024,512]{1,0:T(8,128)} %copy-done.6) | copy-start | bytes 6291460
  153.2 31.9 %copy-start.2 = (f32[64,64,128]{2,1,0:T(8,128)S(1)}, f32[64,64,128]{2,1,0:T(8,128)}, u32[]{:S(2)}) copy-start(f32[64,64,128]{2,1,0:T(8,128)} %param.6) | copy-start | bytes 6291460
  166.9 126.4 %all-to-all-start.3 = ((f32[8,128,512]{1,0,2:T(8,128)}), f32[8,128,512]{1,0,2:T(8,128)}, u32[]{:S(2)}, u32[]{:S(2)}) async-start(f32[8,128,512]{1,0,2:T(8,128)} %copy.25), calls=%async_computation.3 | async-start | bytes 4194304 | tf_op jit(solution)/shard_map/all_to_all | solution.py:125
  194.6 17.0 %collective-permute-start = (f32[2,64,64,1]{2,1,3,0:T(8,128)S(1)}, f32[2,64,64,1]{2,1,3,0:T(8,128)S(1)}, u32[]{:S(2)}, u32[]{:S(2)}) collective-permute-start(f32[2,64,64,1]{2,1,3,0:T(8,128)S(1)} %copy.30), channel_id=1, source_target_pairs={{0,64},{64,128},{128,192},{1,65},{65,129},{129,193},{2,66},{66,130... | collective-permute-start | bytes 98312 | tf_op jit(solution)/shard_map/ppermute | solution.py:26
  201.8 37.7 %collective-permute-start.1 = (f32[2,64,64,1]{2,1,3,0:T(8,128)S(1)}, f32[2,64,64,1]{2,1,3,0:T(8,128)S(1)}, u32[]{:S(2)}, u32[]{:S(2)}) collective-permute-start(f32[2,64,64,1]{2,1,3,0:T(8,128)S(1)} %copy.31), channel_id=1, source_target_pairs={{64,0},{128,64},{192,128},{65,1},{129,65},{193,129},{66,2},{130,66... | collective-permute-start | bytes 98312 | tf_op jit(solution)/shard_map/ppermute | solution.py:27
  242.2 12.3 %copy-start = (f32[2,64,64,1]{3,2,1,0:T(8,128)S(1)}, f32[2,64,64,1]{3,2,1,0:T(8,128)}, u32[]{:S(2)}) copy-start(f32[2,64,64,1]{3,2,1,0:T(8,128)} %copy.32) | copy-start | bytes 98308
  242.3 12.3 %copy-start.1 = (f32[2,64,64,1]{3,2,1,0:T(8,128)S(1)}, f32[2,64,64,1]{3,2,1,0:T(8,128)}, u32[]{:S(2)}) copy-start(f32[2,64,64,1]{3,2,1,0:T(8,128)} %copy.33) | copy-start | bytes 98308
  242.3 12.3 %copy-start.3 = (f32[64,64,128]{2,1,0:T(8,128)S(1)}, f32[64,64,128]{2,1,0:T(8,128)}, u32[]{:S(2)}) copy-start(f32[64,64,128]{2,1,0:T(8,128)} %param.7) | copy-start | bytes 6291460
  243.5 4.2 %collective-permute-start.2 = (f32[2,1,64,130]{3,2,1,0:T(8,128)S(1)}, f32[2,1,64,130]{3,2,1,0:T(8,128)S(1)}, u32[]{:S(2)}, u32[]{:S(2)}) collective-permute-start(f32[2,1,64,130]{3,2,1,0:T(8,128)S(1)} %get-tuple-element.9), channel_id=1, source_target_pairs={{0,8},{8,16},{16,24},{24,32},{32,40},{40,48},{48,56},{1,9},{9,17},... | collective-permute-start | bytes 199688 | tf_op jit(solution)/shard_map/ppermute | solution.py:26
  245.1 9.5 %collective-permute-start.3 = (f32[2,1,64,130]{3,2,1,0:T(8,128)S(1)}, f32[2,1,64,130]{3,2,1,0:T(8,128)S(1)}, u32[]{:S(2)}, u32[]{:S(2)}) collective-permute-start(f32[2,1,64,130]{3,2,1,0:T(8,128)S(1)} %get-tuple-element.10), channel_id=1, source_target_pairs={{8,0},{16,8},{24,16},{32,24},{40,32},{48,40},{56,48},{9,1},{17,9},... | collective-permute-start | bytes 199688 | tf_op jit(solution)/shard_map/ppermute | solution.py:27
  255.5 4.6 %collective-permute-start.4 = (f32[2,66,1,130]{3,2,1,0:T(1,128)S(1)}, f32[2,66,1,130]{3,2,1,0:T(1,128)S(1)}, u32[]{:S(2)}, u32[]{:S(2)}) collective-permute-start(f32[2,66,1,130]{3,2,1,0:T(1,128)S(1)} %get-tuple-element.7), channel_id=1, source_target_pairs={{0,1},{1,2},{2,3},{3,4},{4,5},{5,6},{6,7},{8,9},{9,10},{10,11},{11... | collective-permute-start | bytes 205928 | tf_op jit(solution)/shard_map/ppermute | solution.py:26
  258.0 6.3 %collective-permute-start.5 = (f32[2,66,1,130]{3,2,1,0:T(1,128)S(1)}, f32[2,66,1,130]{3,2,1,0:T(1,128)S(1)}, u32[]{:S(2)}, u32[]{:S(2)}) collective-permute-start(f32[2,66,1,130]{3,2,1,0:T(1,128)S(1)} %get-tuple-element.8), channel_id=1, source_target_pairs={{1,0},{2,1},{3,2},{4,3},{5,4},{6,5},{7,6},{9,8},{10,9},{11,10},{12... | collective-permute-start | bytes 205928 | tf_op jit(solution)/shard_map/ppermute | solution.py:27
  314.2 18.7 %slice-start = ((s8[4866048]{0:T(1024)(128)(4,1)}), s8[671744]{0:T(1024)(128)(4,1)S(1)}, s32[]{:S(2)}) async-start(s8[4866048]{0:T(1024)(128)(4,1)} %bitcast.57), calls=%async_computation.5 | async-start | bytes 1343488
  314.2 29.4 %all-to-all-start.4 = ((f32[8,512,128]{2,0,1:T(8,128)}), f32[8,512,128]{2,0,1:T(8,128)}, u32[]{:S(2)}, u32[]{:S(2)}) async-start(f32[8,512,128]{2,0,1:T(8,128)} %copy.27), calls=%async_computation.4 | async-start | bytes 4194304 | tf_op jit(solution)/shard_map/all_to_all | solution.py:128
  318.6 14.3 %slice-start.1 = ((s8[4866048]{0:T(1024)(128)(4,1)}), s8[4194304]{0:T(1024)(128)(4,1)S(1)}, s32[]{:S(2)}) async-start(s8[4866048]{0:T(1024)(128)(4,1)} %bitcast.57), calls=%async_computation.6 | async-start | bytes 8388608
where the time goes:
time: 363 us; the launch traced here: 357 us
  matrix products  90.9 us (25%)
  waiting for transfers between devices  84.4 us (23%)
  starting transfers between devices  71.9 us (20%)
  local copies, waits for them, and re-layouts  62.9 us (17%)
  other arithmetic  46.2 us (13%)
    ppermute x3, waiting for transfers between devices, padded_2(): after = lax.ppermute(initial, axis, down)  36.3 us
    all_to_all x1, starting transfers between devices, on_device(): lax.all_to_all(imag_part, 'gx', split_axis=2, concat_axis=1, tiled=True)  18.2 us
    all_to_all x1, starting transfers between devices, on_device(): lax.all_to_all(imag_part, ('gy', 'gz'), split_axis=0, concat_axis=1, tile...  17.8 us
    mul x1, other arithmetic, on_device(): flux_y = scaled * slope_y  14.3 us
    all_to_all x1, waiting for transfers between devices, on_device(): lax.all_to_all(real_part, 'gx', split_axis=2, concat_axis=1, tiled=True)  13.7 us
    all_to_all x1, waiting for transfers between devices, on_device(): lax.all_to_all(imag_part, ('gy', 'gz'), split_axis=0, concat_axis=1, tile...  13.2 us
    sub x1, other arithmetic, on_device(): return volume - step_size * (data_term + tv_weight * tv_grad)  11.2 us
    dot_general x1, matrix products, depth_transform(): jnp.einsum('nk,ykx->ynx', sin_depth, imag_in, precision=highest, preferre...  10.6 us
  transfers between devices with their start and end apart: 11, of which 9 were waited for; matrix products, arithmetic and copies ran while one was open for 34% of the time, Pallas kernels for 0%

commit v1 on v0

v1 whole, which is shorter than its diff:
```python
import functools
import math

import jax
import jax.numpy as jnp
import ml_dtypes
import numpy as np
from jax import lax
from jax.experimental import pallas as pl
from jax.experimental.pallas import tpu as pltpu
from jax.sharding import PartitionSpec as P

step_size = 0.5
tv_weight = 0.5
smoothing = 0.5
MESH = pl.DeviceIdType.MESH
X_CHIPS = 4


def padded_2(x, sides, width):
    for axis, dim in sides:
        size, length = (lax.axis_size(axis), x.shape[dim])
        up = [(i, (i + 1) % size) for i in range(size - 1)]
        down = [(j, i) for i, j in up]
        last = lax.slice_in_dim(x, length - width, length, axis=dim)
        initial = lax.slice_in_dim(x, 0, width, axis=dim)
        before = lax.ppermute(last, axis, up)
        after = lax.ppermute(initial, axis, down)
        x = jnp.concatenate([before, x, after], axis=dim)
    return x


def region(field, start_y, start_z, start_x, size_y, size_z, size_x):
    return field[start_y : start_y + size_y, start_z : start_z + size_z, start_x : start_x + size_x]


def tv_gradient(volume, weights):
    stacked = jnp.stack([volume, weights])
    padded = padded_2(stacked, (("gx", 3), ("gy", 1), ("gz", 2)), 1)
    brick_y, brick_z, brick_x = volume.shape
    end_y, end_z, end_x = (n * lax.axis_size(a) for n, a in zip(volume.shape, ("gy", "gz", "gx")))
    span_y, span_z, span_x = (brick_y + 1, brick_z + 1, brick_x + 1)
    field = padded[0]
    edge_weights = padded[1]
    base = region(field, 0, 0, 0, span_y, span_z, span_x)
    global_y = lax.axis_index("gy") * brick_y + jnp.arange(span_y, dtype=jnp.int32) - 1
    global_z = lax.axis_index("gz") * brick_z + jnp.arange(span_z, dtype=jnp.int32) - 1
    global_x = lax.axis_index("gx") * brick_x + jnp.arange(span_x, dtype=jnp.int32) - 1
    slope_y = region(field, 1, 0, 0, span_y, span_z, span_x) - base
    slope_z = region(field, 0, 1, 0, span_y, span_z, span_x) - base
    slope_x = region(field, 0, 0, 1, span_y, span_z, span_x) - base
    slope_y = jnp.where((global_y < end_y - 1)[:, None, None], slope_y, 0.0)
    slope_z = jnp.where((global_z < end_z - 1)[None, :, None], slope_z, 0.0)
    slope_x = jnp.where((global_x < end_x - 1)[None, None, :], slope_x, 0.0)
    magnitude = jnp.sqrt(slope_y * slope_y + slope_z * slope_z + slope_x * slope_x + smoothing)
    inside = (
        (global_y >= 0)[:, None, None]
        & (global_z >= 0)[None, :, None]
        & (global_x >= 0)[None, None, :]
    )
    scaled = jnp.where(
        inside, region(edge_weights, 0, 0, 0, span_y, span_z, span_x) / magnitude, 0.0
    )
    flux_y = scaled * slope_y
    flux_z = scaled * slope_z
    flux_x = scaled * slope_x
    tv_grad = flux_y[:-1, 1:, 1:] - flux_y[1:, 1:, 1:]
    tv_grad = tv_grad + flux_z[1:, :-1, 1:] - flux_z[1:, 1:, 1:]
    tv_grad = tv_grad + flux_x[1:, 1:, :-1] - flux_x[1:, 1:, 1:]
    return tv_grad


def halves(table):
    high = table.astype(ml_dtypes.bfloat16)
    low = (table - high.astype(np.float64)).astype(ml_dtypes.bfloat16)
    return np.stack([high, low])


def cos_sin(length, rows, columns):
    phases = (np.asarray(rows)[:, None] * np.asarray(columns)[None, :]) % length
    angles = phases * (2.0 * math.pi / length)
    factor = 1.0 / math.sqrt(length)
    return np.cos(angles) * factor, np.sin(angles) * factor


class Sizes:
    def __init__(self, mesh_sizes, x_chips, ny, nz, nx):
        self.gx, self.gy, self.gz = mesh_sizes
        self.ny, self.nz, self.nx = ny, nz, nx
        self.plane = self.gx * self.gy
        self.planes = nz // (self.plane * self.gz)
        self.chips = x_chips
        self.ring = self.plane // x_chips
        self.by, self.bz, self.bx = ny // self.gy, nz // self.gz, nx // self.gx
        self.rows = self.by // self.gz
        self.lines = 2 * nz


def make_tables(s):
    c, n = cos_sin(s.nx, range(s.nx), range(s.nx))
    table_x = halves(np.concatenate([c, n], axis=0))
    c, n = cos_sin(s.ny, range(s.ny), range(s.ny))
    table_y = halves(np.concatenate([c, n], axis=1))
    k, r, g, x = np.meshgrid(
        range(s.planes), range(s.ring), range(s.gz), range(s.chips), indexing="ij"
    )
    kz = (((r * s.chips + x) * s.gz + g) * s.planes + k).reshape(-1)
    c, n = cos_sin(s.nz, range(s.nz), kz)
    table_z = halves(np.stack([c, -n], axis=-1).reshape(s.nz, s.lines))
    return table_x, table_y, table_z


def split(x):
    high = x.astype(jnp.bfloat16)
    return high, (x - high.astype(jnp.float32)).astype(jnp.bfloat16)


def dot3(a_high, a_low, b_high, b_low):
    f32 = jnp.float32
    return (
        jnp.dot(a_high, b_high, preferred_element_type=f32)
        + jnp.dot(a_high, b_low, preferred_element_type=f32)
        + jnp.dot(a_low, b_high, preferred_element_type=f32)
    )


def kernel(
    s, sr, si, tx, ty, tz, out,
    mid, mine, blocks, pencils, lines, bricks,
    send1, recv1, send2, recv2, send3, recv3,
):
    gx, gy, gz = lax.axis_index("gx"), lax.axis_index("gy"), lax.axis_index("gz")
    here = gx * s.gy + gy
    ring, chip = here // s.chips, here % s.chips
    half = s.nx
    lanes = s.nx // 128
    tile_y = min(256, s.ny)
    chunk = min(128, s.ny)

    def place(index):
        return (index // s.gy, index % s.gy, gz)

    def beside(step):
        return (gx, gy, (gz + step) % s.gz)

    barrier = pltpu.get_barrier_semaphore()

    def greet(i, _):
        pl.semaphore_signal(barrier, inc=1, device_id=place((here + i) % s.plane), device_id_type=MESH)
        return 0

    def greet_beside(i, _):
        pl.semaphore_signal(barrier, inc=1, device_id=beside(i), device_id_type=MESH)
        return 0

    lax.fori_loop(1, s.plane, greet, 0)
    lax.fori_loop(1, s.gz, greet_beside, 0)

    def transform_x(k):
        def body(t, _):
            def plane_rows(ref):
                first = t * chunk * lanes * s.planes + k
                return jnp.concatenate(
                    [
                        ref[pl.ds(first + j * s.planes, chunk, stride=lanes * s.planes), :]
                        for j in range(lanes)
                    ],
                    axis=1,
                )

            re_high, re_low = split(plane_rows(sr))
            im_high, im_low = split(plane_rows(si))
            high = jnp.concatenate(
                [jnp.concatenate([re_high, -im_high], 1), jnp.concatenate([im_high, re_high], 1)], 0
            )
            low = jnp.concatenate(
                [jnp.concatenate([re_low, -im_low], 1), jnp.concatenate([im_low, re_low], 1)], 0
            )
            both = dot3(high, low, tx[0], tx[1])
            re_high, re_low = split(both[:chunk])
            im_high, im_low = split(both[chunk:])
            at = pl.multiple_of(t * chunk, chunk)
            mid[0, pl.ds(at, chunk), :] = im_high
            mid[1, pl.ds(at, chunk), :] = im_low
            mid[0, pl.ds(s.ny + at, chunk), :] = re_high
            mid[1, pl.ds(s.ny + at, chunk), :] = re_low
            mid[0, pl.ds(2 * s.ny + at, chunk), :] = -im_high
            mid[1, pl.ds(2 * s.ny + at, chunk), :] = -im_low
            return 0

        lax.fori_loop(0, s.ny // chunk, body, 0)

    def transform_y(k):
        per = tile_y // s.by

        def body(t, _):
            at = pl.multiple_of(t * tile_y, tile_y)
            high, low = ty[0, pl.ds(at, tile_y), :], ty[1, pl.ds(at, tile_y), :]
            for c, first in ((0, s.ny), (1, 0)):
                o = dot3(
                    high, low, mid[0, first : first + 2 * s.ny, :], mid[1, first : first + 2 * s.ny, :]
                )
                for q in range(s.gx):
                    mine[pl.ds(q * s.gy + t * per, per), k, c] = o[
                        :, q * 128 : (q + 1) * 128
                    ].reshape(per, s.by, 128)
            return 0

        lax.fori_loop(0, s.ny // tile_y, body, 0)

    turns = []
    for h in range(1, s.ring // 2 + 1):
        turns += [h] if 2 * h == s.ring else [h, s.ring - h]

    def send_block(k, turn, dx):
        to = ((ring + turn) % s.ring) * s.chips + (chip + dx) % s.chips
        pltpu.make_async_remote_copy(
            src_ref=mine.at[to, k],
            dst_ref=blocks.at[k, pl.ds(2 * here, 2)],
            send_sem=send1,
            recv_sem=recv1.at[k, ring],
            device_id=place(to),
            device_id_type=MESH,
        ).start()

    def plane(k, _):
        transform_x(k)
        transform_y(k)

        @pl.when(k == 0)
        def _():
            pl.semaphore_wait(barrier, s.plane - 1 + s.gz - 1)

        for turn in turns:
            lax.fori_loop(0, s.chips, lambda dx, _: (send_block(k, turn, dx), 0)[1], 0)
        lax.fori_loop(1, s.chips, lambda dx, _: (send_block(k, 0, dx), 0)[1], 0)
        pltpu.make_async_copy(
            mine.at[here, k], blocks.at[k, pl.ds(2 * here, 2)], recv1.at[k, ring]
        ).start()
        return 0

    lax.fori_loop(0, s.planes, plane, 0)

    width = 2 * s.chips

    def forward(k, _):
        for turn in turns + [0]:
            source = (ring + s.ring - turn) % s.ring
            group = blocks.at[k, pl.ds(source * width, width)]
            pltpu.make_async_copy(group, group, recv1.at[k, source]).wait()

            def step(i, _):
                to = (gz + i) % s.gz
                pltpu.make_async_remote_copy(
                    src_ref=group.at[:, pl.ds(to * s.rows, s.rows), :],
                    dst_ref=pencils.at[pl.ds(((k * s.ring + source) * s.gz + gz) * width, width)],
                    send_sem=send2,
                    recv_sem=recv2,
                    device_id=beside(i),
                    device_id_type=MESH,
                ).start()
                return 0

            lax.fori_loop(1, s.gz, step, 0)
            pltpu.make_async_copy(
                group.at[:, pl.ds(gz * s.rows, s.rows), :],
                pencils.at[pl.ds(((k * s.ring + source) * s.gz + gz) * width, width)],
                recv2,
            ).start()
        return 0

    lax.fori_loop(0, s.planes, forward, 0)
    pltpu.make_async_copy(pencils, pencils, recv2).wait()

    tile_z = min(256, s.nz)

    def transform_z(pair, _):
        pieces = [
            split(pencils[:, 2 * pair + j, :]) for j in range(2)
        ]
        high = jnp.concatenate([p[0] for p in pieces], axis=1)
        low = jnp.concatenate([p[1] for p in pieces], axis=1)
        for t in range(s.nz // tile_z):
            at = slice(t * tile_z, (t + 1) * tile_z)
            o = dot3(tz[0, at, :], tz[1, at, :], high, low)
            for j in range(2):
                lines[2 * pair + j, at, :] = o[:, j * 128 : (j + 1) * 128]

        def step(i, _):
            to = (gz + i) % s.gz
            pltpu.make_async_remote_copy(
                src_ref=lines.at[pl.ds(2 * pair, 2), pl.ds(to * s.bz, s.bz), :],
                dst_ref=bricks.at[gz, pl.ds(2 * pair, 2)],
                send_sem=send3,
                recv_sem=recv3,
                device_id=beside(i),
                device_id_type=MESH,
            ).start()
            return 0

        lax.fori_loop(1, s.gz, step, 0)
        pltpu.make_async_copy(
            lines.at[pl.ds(2 * pair, 2), pl.ds(gz * s.bz, s.bz), :],
            bricks.at[gz, pl.ds(2 * pair, 2)],
            recv3,
        ).start()
        return 0

    lax.fori_loop(0, s.rows // 2, transform_z, 0)
    pltpu.make_async_copy(bricks, bricks, recv3).wait()
    out[...] = bricks[...].reshape(out.shape)

    sent = mine.at[pl.ds(0, s.plane - 1)]
    pltpu.make_async_copy(sent, sent, send1).wait()
    sent = pencils.at[pl.ds(0, s.lines // s.gz * (s.gz - 1))]
    pltpu.make_async_copy(sent, sent, send2).wait()
    sent = bricks.at[pl.ds(0, s.gz - 1)]
    pltpu.make_async_copy(sent, sent, send3).wait()


def data_term(s, spectrum_real, spectrum_imag):
    tables = make_tables(s)

    def rows(x):
        x = x.reshape(s.ny, s.planes, s.nx // 128, 128)
        return x.transpose(0, 2, 1, 3).reshape(-1, 128)

    f32 = jnp.float32
    return pl.pallas_call(
        functools.partial(kernel, s),
        out_shape=jax.ShapeDtypeStruct((s.by, s.bz, s.bx), f32),
        in_specs=[pl.BlockSpec(memory_space=pltpu.VMEM)] * 5,
        out_specs=pl.BlockSpec(memory_space=pltpu.VMEM),
        scratch_shapes=[
            pltpu.VMEM((2, 3 * s.ny, s.nx), jnp.bfloat16),
            pltpu.VMEM((s.plane, s.planes, 2, s.by, 128), f32),
            pltpu.VMEM((s.planes, 2 * s.plane, s.by, 128), f32),
            pltpu.VMEM((s.lines, s.rows, 128), f32),
            pltpu.VMEM((s.rows, s.nz, 128), f32),
            pltpu.VMEM((s.gz, s.rows, s.bz, 128), f32),
            pltpu.SemaphoreType.DMA,
            pltpu.SemaphoreType.DMA((s.planes, s.ring)),
            pltpu.SemaphoreType.DMA,
            pltpu.SemaphoreType.DMA,
            pltpu.SemaphoreType.DMA,
            pltpu.SemaphoreType.DMA,
        ],
        compiler_params=pltpu.CompilerParams(
            collective_id=0, has_side_effects=True, vmem_limit_bytes=60 * 1024 * 1024
        ),
    )(rows(spectrum_real), rows(spectrum_imag), *(jnp.asarray(t) for t in tables))


def on_device(s, spectrum_real, spectrum_imag, volume, weights):
    tv_grad = tv_gradient(volume, weights)
    data = data_term(s, spectrum_real, spectrum_imag)
    return volume - step_size * (data + tv_weight * tv_grad)


def build(mesh, x_chips, shape):
    sizes = Sizes([mesh.shape[a] for a in ("gx", "gy", "gz")], x_chips, *shape)
    spectrum, brick = P(None, ("gx", "gy", "gz"), None), P("gy", "gz", "gx")
    return jax.shard_map(
        functools.partial(on_device, sizes),
        mesh=mesh,
        in_specs=(spectrum, spectrum, brick, brick),
        out_specs=brick,
        check_vma=False,
    )


def solution(mesh):
    return build(mesh, X_CHIPS, (512, 512, 512))
```

time: 363 us -> 225 us (0.62); the launches traced: 357 us -> 223 us
  Pallas kernels: 0 us -> 149 us
  matrix products: 90.9 us -> 0 us
  waiting for transfers between devices: 84.4 us -> 9.62 us
  starting transfers between devices: 71.9 us -> 16.2 us
  local copies, waits for them, and re-layouts: 62.9 us -> 14.2 us
  other arithmetic: 46.2 us -> 33.5 us
    pallas_call x0 -> x1, Pallas kernels: none -> 149 us  [data_term(): pl.pallas_call(functools.partial(kernel, s), out_shape=jax.ShapeDtypeStru...]
    dot_general x10 -> x0, matrix products: 90.9 us -> none  [the longest x1 10.6 us: depth_transform(): jnp.einsum('nk,ykx->ynx', sin_depth, imag_in, precision=highest, preferre...]
    all_to_all x5 -> x0, starting transfers between devices: 58.7 us -> none  [the longest x1 18.2 us: on_device(): lax.all_to_all(imag_part, 'gx', split_axis=2, concat_axis=1, tiled=True)]
    all_to_all x5 -> x0, waiting for transfers between devices: 38.7 us -> none  [the longest x1 13.7 us: on_device(): lax.all_to_all(real_part, 'gx', split_axis=2, concat_axis=1, tiled=True)]
    ppermute x3, waiting for transfers between devices: 36.3 us -> 7.85 us  [padded_2(): after = lax.ppermute(initial, axis, down)]
    all_to_all x9 -> x0, local copies, waits for them, and re-layouts: 23.6 us -> none  [the longest x2 7.34 us: on_device(): lax.all_to_all(real_part, 'gx', split_axis=2, concat_axis=1, tiled=True)]
    reshape x6 -> x0, local copies, waits for them, and re-layouts: 16.7 us -> none  [the longest x1 4.01 us: on_device(): imag_part = (jnp.dot(sin_rows, flat_real, precision=highest) + jnp.dot(co...]
    mul x2, other arithmetic: 18.9 us -> 9.65 us  [the longest x1 6.27 us: tv_gradient(): flux_y = scaled * slope_y]
  transfers between devices with their start and end apart: 11 -> 6, of which waited for: 9 -> 3; matrix products, arithmetic and copies ran while one was open for 34% -> 3% of each run, Pallas kernels for 0% -> 67%
where the time goes in v1:
time: 225 us; the launch traced here: 223 us
  Pallas kernels  149 us (66%)
  other arithmetic  33.5 us (15%)
  starting transfers between devices  16.2 us (7%)
  local copies, waits for them, and re-layouts  14.2 us (6%)
  waiting for transfers between devices  9.62 us (4%)
    pallas_call x1, Pallas kernels, data_term(): pl.pallas_call(functools.partial(kernel, s), out_shape=jax.ShapeDtypeStru...  149 us
    ppermute x3, starting transfers between devices, padded_2(): before = lax.ppermute(last, axis, up)  11.3 us
    ppermute x3, waiting for transfers between devices, padded_2(): after = lax.ppermute(initial, axis, down)  7.85 us
    another operation x1, other arithmetic, tv_gradient(): stacked = jnp.stack([volume, weights])  7.82 us
    concatenate x1, other arithmetic, padded_2(): x = jnp.concatenate([before, x, after], axis=dim)  7.33 us
    sub x1, other arithmetic, on_device(): return volume - step_size * (data + tv_weight * tv_grad)  6.5 us
    mul x1, other arithmetic, tv_gradient(): flux_y = scaled * slope_y  6.27 us
    ppermute x3, starting transfers between devices, padded_2(): after = lax.ppermute(initial, axis, down)  4.95 us
  transfers between devices with their start and end apart: 6, of which 3 were waited for; matrix products, arithmetic and copies ran while one was open for 3% of the time, Pallas kernels for 67%

profile of v1, /device:TPU:1, one launch (start us, length us, event | category | flops | bytes accessed | tf_op | source)
XLA Modules:
  0.0 223.0 jit_solution(13624281507400644138)
XLA Ops:
  0.0 7.8 %slice_maximum_fusion = (f32[2,64,64,1]{3,2,1,0:T(8,128)}, f32[2,64,64,1]{3,2,1,0:T(8,128)}) fusion(f32[1,64,64,128]{3,2,1,0:T(8,128)} %bitcast.20, f32[1,64,64,128]{3,2,1,0:T(8,128)} %bitcast.16), kind=kLoop, calls=%fused_computation.12 | loop fusion | flops 16384 | bytes 4259840 | tf_op jit(solution)/shard_map/stack | solution.py:38
  7.8 3.0 %copy.12 = f32[2,64,64,1]{2,1,3,0:T(8,128)S(1)} copy(f32[2,64,64,1]{3,2,1,0:T(8,128)} %get-tuple-element.15) | data formatting | bytes 65536 | tf_op jit(solution)/shard_map/slice | solution.py:25
  10.8 5.7 %collective-permute-start = (f32[2,64,64,1]{2,1,3,0:T(8,128)S(1)}, f32[2,64,64,1]{2,1,3,0:T(8,128)S(1)}, u32[]{:S(2)}, u32[]{:S(2)}) collective-permute-start(f32[2,64,64,1]{2,1,3,0:T(8,128)S(1)} %copy.12), channel_id=1, source_target_pairs={{0,64},{64,128},{128,192},{1,65},{65,129},{129,193},{2,66},{66,130... | collective-permute-start | bytes 98312 | tf_op jit(solution)/shard_map/ppermute | solution.py:27
  16.5 3.0 %copy.13 = f32[2,64,64,1]{2,1,3,0:T(8,128)S(1)} copy(f32[2,64,64,1]{3,2,1,0:T(8,128)} %get-tuple-element.16) | data formatting | bytes 65536 | tf_op jit(solution)/shard_map/slice | solution.py:26
  19.5 1.3 collective-permute-start.1
  20.8 0.1 broadcast_and_fusion
  20.9 149.3 %shard_map.73 = f32[64,64,128]{2,1,0:T(8,128)} custom-call(f32[4096,128]{1,0:T(8,128)} %bitcast.24, f32[4096,128]{1,0:T(8,128)} %bitcast.25, bf16[2,1024,512]{2,1,0:T(8,128)(2,1)} %constant.39.clone.tx, bf16[2,512,1024]{2,1,0:T(8,128)(2,1)} %constant.40.clone.ty, bf16[2,512,1024]{2,1,0:T(8,128)(2,1)} %constant.41.clone.tz), custom_call_target="tpu_custom_call" | custom-call | tf_op jit(solution)/shard_map/pallas_call | solution.py:329
  170.2 0.0 copy-start.2
  170.2 0.0 collective-permute-done
  170.2 2.8 %copy.14 = f32[2,64,64,1]{3,2,1,0:T(8,128)} copy(f32[2,64,64,1]{2,1,3,0:T(8,128)S(1)} %collective-permute-done) | data formatting | bytes 65536 | tf_op jit(solution)/shard_map/ppermute | solution.py:27
  173.0 0.0 collective-permute-done.1
  173.0 2.7 %copy.15 = f32[2,64,64,1]{3,2,1,0:T(8,128)} copy(f32[2,64,64,1]{2,1,3,0:T(8,128)S(1)} %collective-permute-done.1) | data formatting | bytes 65536 | tf_op jit(solution)/shard_map/ppermute | solution.py:28
  175.7 0.0 copy-done.2
  175.7 0.0 copy-start
  175.7 0.0 copy-start.1
  175.7 0.0 copy-start.3
  175.7 1.3 pad_maximum_fusion.11
  176.9 3.4 %collective-permute-start.2 = (f32[2,1,64,130]{3,2,1,0:T(8,128)S(1)}, f32[2,1,64,130]{3,2,1,0:T(8,128)S(1)}, u32[]{:S(2)}, u32[]{:S(2)}) collective-permute-start(f32[2,1,64,130]{3,2,1,0:T(8,128)S(1)} %get-tuple-element.9), channel_id=1, source_target_pairs={{0,8},{8,16},{16,24},{24,32},{32,40},{40,48},{48,56},{1,9},{9,17},... | collective-permute-start | bytes 199688 | tf_op jit(solution)/shard_map/ppermute | solution.py:27
  180.3 1.3 collective-permute-start.3
  181.7 1.8 collective-permute-done.2
  183.4 3.9 %collective-permute-done.3 = f32[2,1,64,130]{3,2,1,0:T(8,128)S(1)} collective-permute-done((f32[2,1,64,130]{3,2,1,0:T(8,128)S(1)}, f32[2,1,64,130]{3,2,1,0:T(8,128)S(1)}, u32[]{:S(2)}, u32[]{:S(2)}) %collective-permute-start.3) | collective-permute-done | bytes 66592 | tf_op jit(solution)/shard_map/ppermute | solution.py:28
  187.3 0.0 copy-done
  187.3 0.0 copy-done.1
  187.3 0.0 copy-done.3
  187.3 0.9 pad_maximum_fusion.7
  188.2 2.2 collective-permute-start.4
  190.4 2.4 %collective-permute-start.5 = (f32[2,66,1,130]{3,2,1,0:T(1,128)S(1)}, f32[2,66,1,130]{3,2,1,0:T(1,128)S(1)}, u32[]{:S(2)}, u32[]{:S(2)}) collective-permute-start(f32[2,66,1,130]{3,2,1,0:T(1,128)S(1)} %get-tuple-element.8), channel_id=1, source_target_pairs={{1,0},{2,1},{3,2},{4,3},{5,4},{6,5},{7,6},{9,8},{10,9},{11,10},{12... | collective-permute-start | bytes 205928 | tf_op jit(solution)/shard_map/ppermute | solution.py:28
  192.8 0.0 collective-permute-done.4
  192.8 3.9 %collective-permute-done.5 = f32[2,66,1,130]{3,2,1,0:T(1,128)S(1)} collective-permute-done((f32[2,66,1,130]{3,2,1,0:T(1,128)S(1)}, f32[2,66,1,130]{3,2,1,0:T(1,128)S(1)}, u32[]{:S(2)}, u32[]{:S(2)}) %collective-permute-start.5) | collective-permute-done | bytes 68672 | tf_op jit(solution)/shard_map/ppermute | solution.py:28
  196.7 7.3 %pad_maximum_fusion = f32[2,66,66,130]{3,2,1,0:T(8,128)S(1)} fusion(f32[2,66,1,130]{3,2,1,0:T(1,128)S(1)} %collective-permute-done.5, f32[2,1,64,130]{3,2,1,0:T(8,128)S(1)} %collective-permute-done.3, f32[2,64,64,1]{3,2,1,0:T(8,128)S(1)} %copy-done.1, f32[1,64,64,128]{3,2,1,0:T(8,128)S(1)} %bitcast.23, f32[1,64,64,128]{3,2,1,0:T(8,128)S(1)} %bitcast.19, ...), kind=kLoop, calls=%fused_computation | loop fusion | flops 7927920 | bytes 9060480 | tf_op jit(solution)/shard_map/concatenate | solution.py:29
  204.1 2.8 %slice_bitcast_fusion.1 = (f32[66,66,130]{2,1,0:T(8,128)}, f32[66,66,130]{2,1,0:T(8,128)S(1)}) fusion(f32[2,66,66,130]{3,2,1,0:T(8,128)S(1)} %pad_maximum_fusion), kind=kLoop, calls=%fused_computation.2 | loop fusion | bytes 9060480 | tf_op jit(solution)/shard_map/squeeze | solution.py:44
  206.9 6.3 %fusion.9 = (f32[65,65,129]{2,1,0:T(8,128)S(1)}, f32[65,65,129]{2,1,0:T(8,128)S(1)}) fusion(f32[66,66,130]{2,1,0:T(8,128)S(1)} %get-tuple-element.12, pred[65]{0:T(512)(128)(4,1)S(1)} %get-tuple-element.21, pred[129]{0:T(512)(128)(4,1)S(1)} %get-tuple-element.17, pred[65]{0:T(512)(128)(4,1)S(1)} %get-tuple-element.22, f32[66,66,130]{2,1,0:T(8,128)} %get-tuple-element.11, ...), kind=kLoop, calls=%fused_computation.33 | loop fusion | flops 8720400 | bytes 15265313 | tf_op jit(solution)/shard_map/mul | solution.py:64
  213.2 0.0 copy-start.4
  213.2 3.4 %fusion.10 = (f32[65,65,129]{2,1,0:T(8,128)S(1)}, f32[65,65,129]{2,1,0:T(8,128)}) fusion(f32[65,65,129]{2,1,0:T(8,128)S(1)} %get-tuple-element.6, f32[66,66,130]{2,1,0:T(8,128)S(1)} %get-tuple-element.12, pred[65]{0:T(512)(128)(4,1)S(1)} %get-tuple-element.22, pred[129]{0:T(512)(128)(4,1)S(1)} %get-tuple-element.17), kind=kLoop, calls=%fused_computation.34 | loop fusion | flops 3270150 | bytes 13080794 | tf_op jit(solution)/shard_map/mul | solution.py:65
  216.5 0.0 copy-done.4
  216.5 6.5 %fusion.7 = f32[64,64,128]{2,1,0:T(8,128)} fusion(f32[64,64,128]{2,1,0:T(8,128)S(1)} %copy-done.2, f32[64,64,128]{2,1,0:T(8,128)S(1)} %copy-done.4, f32[65,65,129]{2,1,0:T(8,128)} %get-tuple-element.14, f32[65,65,129]{2,1,0:T(8,128)S(1)} %get-tuple-element.13, f32[65,65,129]{2,1,0:T(8,128)S(1)} %get-tuple-element.5), kind=kLoop, calls=%fused_computation.17 | loop fusion | flops 4718592 | bytes 18874368 | tf_op jit(solution)/shard_map/sub | solution.py:357
  (3 shorter events, 0.0 us)
Async XLA Ops:
  10.8 159.4 %collective-permute-start = (f32[2,64,64,1]{2,1,3,0:T(8,128)S(1)}, f32[2,64,64,1]{2,1,3,0:T(8,128)S(1)}, u32[]{:S(2)}, u32[]{:S(2)}) collective-permute-start(f32[2,64,64,1]{2,1,3,0:T(8,128)S(1)} %copy.12), channel_id=1, source_target_pairs={{0,64},{64,128},{128,192},{1,65},{65,129},{129,193},{2,66},{66,130... | collective-permute-start | bytes 98312 | tf_op jit(solution)/shard_map/ppermute | solution.py:27
  19.5 153.5 %collective-permute-start.1 = (f32[2,64,64,1]{2,1,3,0:T(8,128)S(1)}, f32[2,64,64,1]{2,1,3,0:T(8,128)S(1)}, u32[]{:S(2)}, u32[]{:S(2)}) collective-permute-start(f32[2,64,64,1]{2,1,3,0:T(8,128)S(1)} %copy.13), channel_id=1, source_target_pairs={{64,0},{128,64},{192,128},{65,1},{129,65},{193,129},{66,2},{130,66... | collective-permute-start | bytes 98312 | tf_op jit(solution)/shard_map/ppermute | solution.py:28
  170.2 5.5 %copy-start.2 = (f32[64,64,128]{2,1,0:T(8,128)S(1)}, f32[64,64,128]{2,1,0:T(8,128)}, u32[]{:S(2)}) copy-start(f32[64,64,128]{2,1,0:T(8,128)} %param.9) | copy-start | bytes 6291460
  175.7 11.7 %copy-start = (f32[2,64,64,1]{3,2,1,0:T(8,128)S(1)}, f32[2,64,64,1]{3,2,1,0:T(8,128)}, u32[]{:S(2)}) copy-start(f32[2,64,64,1]{3,2,1,0:T(8,128)} %copy.14) | copy-start | bytes 98308
  175.7 11.7 %copy-start.1 = (f32[2,64,64,1]{3,2,1,0:T(8,128)S(1)}, f32[2,64,64,1]{3,2,1,0:T(8,128)}, u32[]{:S(2)}) copy-start(f32[2,64,64,1]{3,2,1,0:T(8,128)} %copy.15) | copy-start | bytes 98308
  175.7 11.7 %copy-start.3 = (f32[64,64,128]{2,1,0:T(8,128)S(1)}, f32[64,64,128]{2,1,0:T(8,128)}, u32[]{:S(2)}) copy-start(f32[64,64,128]{2,1,0:T(8,128)} %param.10) | copy-start | bytes 6291460
  176.9 6.5 %collective-permute-start.2 = (f32[2,1,64,130]{3,2,1,0:T(8,128)S(1)}, f32[2,1,64,130]{3,2,1,0:T(8,128)S(1)}, u32[]{:S(2)}, u32[]{:S(2)}) collective-permute-start(f32[2,1,64,130]{3,2,1,0:T(8,128)S(1)} %get-tuple-element.9), channel_id=1, source_target_pairs={{0,8},{8,16},{16,24},{24,32},{32,40},{40,48},{48,56},{1,9},{9,17},... | collective-permute-start | bytes 199688 | tf_op jit(solution)/shard_map/ppermute | solution.py:27
  180.3 7.0 %collective-permute-start.3 = (f32[2,1,64,130]{3,2,1,0:T(8,128)S(1)}, f32[2,1,64,130]{3,2,1,0:T(8,128)S(1)}, u32[]{:S(2)}, u32[]{:S(2)}) collective-permute-start(f32[2,1,64,130]{3,2,1,0:T(8,128)S(1)} %get-tuple-element.10), channel_id=1, source_target_pairs={{8,0},{16,8},{24,16},{32,24},{40,32},{48,40},{56,48},{9,1},{17,9},... | collective-permute-start | bytes 199688 | tf_op jit(solution)/shard_map/ppermute | solution.py:28
  188.2 4.5 %collective-permute-start.4 = (f32[2,66,1,130]{3,2,1,0:T(1,128)S(1)}, f32[2,66,1,130]{3,2,1,0:T(1,128)S(1)}, u32[]{:S(2)}, u32[]{:S(2)}) collective-permute-start(f32[2,66,1,130]{3,2,1,0:T(1,128)S(1)} %get-tuple-element.7), channel_id=1, source_target_pairs={{0,1},{1,2},{2,3},{3,4},{4,5},{5,6},{6,7},{8,9},{9,10},{10,11},{11... | collective-permute-start | bytes 205928 | tf_op jit(solution)/shard_map/ppermute | solution.py:27
  190.4 6.3 %collective-permute-start.5 = (f32[2,66,1,130]{3,2,1,0:T(1,128)S(1)}, f32[2,66,1,130]{3,2,1,0:T(1,128)S(1)}, u32[]{:S(2)}, u32[]{:S(2)}) collective-permute-start(f32[2,66,1,130]{3,2,1,0:T(1,128)S(1)} %get-tuple-element.8), channel_id=1, source_target_pairs={{1,0},{2,1},{3,2},{4,3},{5,4},{6,5},{7,6},{9,8},{10,9},{11,10},{12... | collective-permute-start | bytes 205928 | tf_op jit(solution)/shard_map/ppermute | solution.py:28
  213.2 3.4 %copy-start.4 = (f32[64,64,128]{2,1,0:T(8,128)S(1)}, f32[64,64,128]{2,1,0:T(8,128)}, u32[]{:S(2)}) copy-start(f32[64,64,128]{2,1,0:T(8,128)} %shard_map.73) | copy-start | bytes 6291460

commit v2 on v1

--- a/solution.py
+++ b/solution.py
@@ -15,59 +15,6 @@
 smoothing = 0.5
 MESH = pl.DeviceIdType.MESH
 X_CHIPS = 4
-
-
-def padded_2(x, sides, width):
-    for axis, dim in sides:
-        size, length = (lax.axis_size(axis), x.shape[dim])
-        up = [(i, (i + 1) % size) for i in range(size - 1)]
-        down = [(j, i) for i, j in up]
-        last = lax.slice_in_dim(x, length - width, length, axis=dim)
-        initial = lax.slice_in_dim(x, 0, width, axis=dim)
-        before = lax.ppermute(last, axis, up)
-        after = lax.ppermute(initial, axis, down)
-        x = jnp.concatenate([before, x, after], axis=dim)
-    return x
-
-
-def region(field, start_y, start_z, start_x, size_y, size_z, size_x):
-    return field[start_y : start_y + size_y, start_z : start_z + size_z, start_x : start_x + size_x]
-
-
-def tv_gradient(volume, weights):
-    stacked = jnp.stack([volume, weights])
-    padded = padded_2(stacked, (("gx", 3), ("gy", 1), ("gz", 2)), 1)
-    brick_y, brick_z, brick_x = volume.shape
-    end_y, end_z, end_x = (n * lax.axis_size(a) for n, a in zip(volume.shape, ("gy", "gz", "gx")))
-    span_y, span_z, span_x = (brick_y + 1, brick_z + 1, brick_x + 1)
-    field = padded[0]
-    edge_weights = padded[1]
-    base = region(field, 0, 0, 0, span_y, span_z, span_x)
-    global_y = lax.axis_index("gy") * brick_y + jnp.arange(span_y, dtype=jnp.int32) - 1
-    global_z = lax.axis_index("gz") * brick_z + jnp.arange(span_z, dtype=jnp.int32) - 1
-    global_x = lax.axis_index("gx") * brick_x + jnp.arange(span_x, dtype=jnp.int32) - 1
-    slope_y = region(field, 1, 0, 0, span_y, span_z, span_x) - base
-    slope_z = region(field, 0, 1, 0, span_y, span_z, span_x) - base
-    slope_x = region(field, 0, 0, 1, span_y, span_z, span_x) - base
-    slope_y = jnp.where((global_y < end_y - 1)[:, None, None], slope_y, 0.0)
-    slope_z = jnp.where((global_z < end_z - 1)[None, :, None], slope_z, 0.0)
-    slope_x = jnp.where((global_x < end_x - 1)[None, None, :], slope_x, 0.0)
-    magnitude = jnp.sqrt(slope_y * slope_y + slope_z * slope_z + slope_x * slope_x + smoothing)
-    inside = (
-        (global_y >= 0)[:, None, None]
-        & (global_z >= 0)[None, :, None]
-        & (global_x >= 0)[None, None, :]
-    )
-    scaled = jnp.where(
-        inside, region(edge_weights, 0, 0, 0, span_y, span_z, span_x) / magnitude, 0.0
-    )
-    flux_y = scaled * slope_y
-    flux_z = scaled * slope_z
-    flux_x = scaled * slope_x
-    tv_grad = flux_y[:-1, 1:, 1:] - flux_y[1:, 1:, 1:]
-    tv_grad = tv_grad + flux_z[1:, :-1, 1:] - flux_z[1:, 1:, 1:]
-    tv_grad = tv_grad + flux_x[1:, 1:, :-1] - flux_x[1:, 1:, 1:]
-    return tv_grad
 
 
 def halves(table):
@@ -125,10 +72,20 @@
 
 
 def kernel(
-    s, sr, si, tx, ty, tz, out,
+    s, sr, si, tx, ty_hbm, tz_hbm, volume_hbm, weights_hbm, out,
     mid, mine, blocks, pencils, lines, bricks,
-    send1, recv1, send2, recv2, send3, recv3,
+    ty, tz, volume, weights, fluxes, faces, halos,
+    face_x, halo_x, flux_face_x, flux_halo_x,
+    send1, recv1, send2, recv2, send3, recv3, load, face_send, face_recv,
 ):
+    late = [
+        pltpu.make_async_copy(source, to, load.at[i])
+        for i, (source, to) in enumerate(
+            ((ty_hbm, ty), (volume_hbm, volume), (weights_hbm, weights), (tz_hbm, tz))
+        )
+    ]
+    for copy in late:
+        copy.start()
     gx, gy, gz = lax.axis_index("gx"), lax.axis_index("gy"), lax.axis_index("gz")
     here = gx * s.gy + gy
     ring, chip = here // s.chips, here % s.chips
@@ -223,8 +180,119 @@
             device_id_type=MESH,
         ).start()
 
+    before_x, after_x = (gx + s.gx - 1) % s.gx, (gx + 1) % s.gx
+    before_y, after_y = (gy + s.gy - 1) % s.gy, (gy + 1) % s.gy
+    flat = s.by * s.bz
+    row_8 = lax.broadcasted_iota(jnp.int32, (8, 128), 0)
+    lane_8 = lax.broadcasted_iota(jnp.int32, (8, 128), 1)
+    lane = lax.broadcasted_iota(jnp.int32, (s.bz, 128), 1)
+    row = lax.broadcasted_iota(jnp.int32, (s.bz, 128), 0)
+
+    def take_lane(ref, which, to):
+        pick = jnp.where(lane_8 == which, 1.0, 0.0)
+        to[...] = lax.dot_general(
+            pick,
+            ref[...].reshape(flat, 128),
+            (((1,), (1,)), ((), ())),
+            precision=lax.Precision.HIGHEST,
+            preferred_element_type=jnp.float32,
+        )[:1]
+
+    def put_lane(ref, which, to):
+        pick = jnp.where((lane_8 == which) & (row_8 == 0), 1.0, 0.0)
+        to[...] = lax.dot_general(
+            jnp.broadcast_to(ref[...], (8, flat)),
+            pick,
+            (((0,), (0,)), ((), ())),
+            precision=lax.Precision.HIGHEST,
+            preferred_element_type=jnp.float32,
+        ).reshape(s.by, s.bz, 128)
+
+    def face_copies(stage, x_from, x_to, to_x, to_y, to_z):
+        pairs = (
+            (x_from, x_to, (to_x, gy, gz)),
+            (faces.at[stage, 0], halos.at[stage, 0], (gx, to_y, gz)),
+            (faces.at[stage, 1], halos.at[stage, 1], (gx, gy, to_z)),
+        )
+        return [
+            pltpu.make_async_remote_copy(
+                src_ref=source,
+                dst_ref=target,
+                send_sem=face_send.at[stage, i],
+                recv_sem=face_recv.at[stage, i],
+                device_id=to,
+                device_id_type=MESH,
+            )
+            for i, (source, target, to) in enumerate(pairs)
+        ]
+
+    volume_faces = face_copies(0, face_x, halo_x, before_x, before_y, (gz + s.gz - 1) % s.gz)
+    flux_faces = face_copies(1, flux_face_x, flux_halo_x, after_x, after_y, (gz + 1) % s.gz)
+
+    def send_faces():
+        take_lane(volume, 0, face_x)
+        faces[0, 0, : s.bz] = volume[0]
+        faces[0, 1, : s.by] = volume[:, 0, :]
+        for copy in volume_faces:
+            copy.start()
+
+    def take_faces():
+        for copy in volume_faces:
+            copy.wait()
+        put_lane(halo_x, 127, fluxes)
+
+    def fluxes_inside():
+        def one(y, v, ahead, x_halo, previous):
+            ahead_z = jnp.where(
+                row == s.bz - 1, halos[0, 1, pl.ds(y, 1), :], pltpu.roll(v, s.bz - 1, 0)
+            )
+            ahead_x = jnp.where(lane == 127, x_halo, pltpu.roll(v, 127, 1))
+            slope_y = ahead - v
+            slope_z = jnp.where((row == s.bz - 1) & (gz == s.gz - 1), 0.0, ahead_z - v)
+            slope_x = jnp.where((lane == 127) & (gx == s.gx - 1), 0.0, ahead_x - v)
+            squares = slope_y * slope_y + slope_z * slope_z + slope_x * slope_x + smoothing
+            scaled = weights[y] * lax.rsqrt(squares)
+            flux_y, flux_z, flux_x = scaled * slope_y, scaled * slope_z, scaled * slope_x
+            gradient = previous - flux_y
+            gradient = gradient + jnp.where(row == 0, 0.0, pltpu.roll(flux_z, 1, 0)) - flux_z
+            gradient = gradient + jnp.where(lane == 0, 0.0, pltpu.roll(flux_x, 1, 1)) - flux_x
+            fluxes[y] = flux_x
+            faces[1, 1, pl.ds(y, 1), :] = flux_z[s.bz - 1 :]
+            out[y] = v - (step_size * tv_weight) * gradient
+            return flux_y
+
+        last = s.by - 1
+        previous = lax.fori_loop(
+            0,
+            last,
+            lambda y, before: one(y, volume[y], volume[y + 1], fluxes[y], before),
+            jnp.zeros((s.bz, 128), jnp.float32),
+        )
+        v = volume[last]
+        ahead = jnp.where(gy == s.gy - 1, v, halos[0, 0, : s.bz])
+        faces[1, 0, : s.bz] = one(last, v, ahead, fluxes[last], previous)
+
+    def send_fluxes():
+        take_lane(fluxes, 127, flux_face_x)
+        for copy in flux_faces:
+            copy.start()
+
+    def take_fluxes():
+        for copy in flux_faces:
+            copy.wait()
+        scale = step_size * tv_weight
+        put_lane(flux_halo_x, 0, fluxes)
+        out[...] = out[...] - jnp.where(gx == 0, 0.0, scale) * fluxes[...]
+        out[0] = out[0] - jnp.where(gy == 0, 0.0, scale) * halos[1, 0, : s.bz]
+        out[:, 0, :] = out[:, 0, :] - jnp.where(gz == 0, 0.0, scale) * halos[1, 1, : s.by]
+
     def plane(k, _):
         transform_x(k)
+
+        @pl.when(k == 0)
+        def _():
+            late[0].wait()
+
         transform_y(k)
 
         @pl.when(k == 0)
@@ -237,6 +305,12 @@
         pltpu.make_async_copy(
             mine.at[here, k], blocks.at[k, pl.ds(2 * here, 2)], recv1.at[k, ring]
         ).start()
+
+        @pl.when(k == 0)
+        def _():
+            late[1].wait()
+            send_faces()
+
         return 0
 
     lax.fori_loop(0, s.planes, plane, 0)
@@ -269,7 +343,14 @@
             ).start()
         return 0
 
-    lax.fori_loop(0, s.planes, forward, 0)
+    for k in range(s.planes):
+        if k == s.planes - 1:
+            late[2].wait()
+            take_faces()
+            fluxes_inside()
+            send_fluxes()
+        forward(k, 0)
+    late[3].wait()
     pltpu.make_async_copy(pencils, pencils, recv2).wait()
 
     tile_z = min(256, s.nz)
@@ -307,8 +388,9 @@
         return 0
 
     lax.fori_loop(0, s.rows // 2, transform_z, 0)
+    take_fluxes()
     pltpu.make_async_copy(bricks, bricks, recv3).wait()
-    out[...] = bricks[...].reshape(out.shape)
+    out[...] = out[...] - step_size * bricks[...].reshape(out.shape)
 
     sent = mine.at[pl.ds(0, s.plane - 1)]
     pltpu.make_async_copy(sent, sent, send1).wait()
@@ -318,43 +400,55 @@
     pltpu.make_async_copy(sent, sent, send3).wait()
 
 
-def data_term(s, spectrum_real, spectrum_imag):
-    tables = make_tables(s)
+def on_device(s, spectrum_real, spectrum_imag, volume, weights):
+    tables = [jnp.asarray(t) for t in make_tables(s)]
 
     def rows(x):
         x = x.reshape(s.ny, s.planes, s.nx // 128, 128)
         return x.transpose(0, 2, 1, 3).reshape(-1, 128)
 
-    f32 = jnp.float32
+    f32, bf16 = jnp.float32, jnp.bfloat16
+    brick = (s.by, s.bz, s.bx)
+    face = max(s.by, s.bz)
+    dma = pltpu.SemaphoreType.DMA
     return pl.pallas_call(
         functools.partial(kernel, s),
-        out_shape=jax.ShapeDtypeStruct((s.by, s.bz, s.bx), f32),
-        in_specs=[pl.BlockSpec(memory_space=pltpu.VMEM)] * 5,
+        out_shape=jax.ShapeDtypeStruct(brick, f32),
+        in_specs=[pl.BlockSpec(memory_space=pltpu.VMEM)] * 3
+        + [pl.BlockSpec(memory_space=pl.ANY)] * 4,
         out_specs=pl.BlockSpec(memory_space=pltpu.VMEM),
         scratch_shapes=[
-            pltpu.VMEM((2, 3 * s.ny, s.nx), jnp.bfloat16),
+            pltpu.VMEM((2, 3 * s.ny, s.nx), bf16),
             pltpu.VMEM((s.plane, s.planes, 2, s.by, 128), f32),
             pltpu.VMEM((s.planes, 2 * s.plane, s.by, 128), f32),
             pltpu.VMEM((s.lines, s.rows, 128), f32),
             pltpu.VMEM((s.rows, s.nz, 128), f32),
             pltpu.VMEM((s.gz, s.rows, s.bz, 128), f32),
-            pltpu.SemaphoreType.DMA,
-            pltpu.SemaphoreType.DMA((s.planes, s.ring)),
-            pltpu.SemaphoreType.DMA,
-            pltpu.SemaphoreType.DMA,
-            pltpu.SemaphoreType.DMA,
-            pltpu.SemaphoreType.DMA,
+            pltpu.VMEM(tables[1].shape, bf16),
+            pltpu.VMEM(tables[2].shape, bf16),
+            pltpu.VMEM(brick, f32),
+            pltpu.VMEM(brick, f32),
+            pltpu.VMEM(brick, f32),
+            pltpu.VMEM((2, 2, face, 128), f32),
+            pltpu.VMEM((2, 2, face, 128), f32),
+            pltpu.VMEM((1, s.by * s.bz), f32),
+            pltpu.VMEM((1, s.by * s.bz), f32),
+            pltpu.VMEM((1, s.by * s.bz), f32),
+            pltpu.VMEM((1, s.by * s.bz), f32),
+            dma,
+            dma((s.planes, s.ring)),
+            dma,
+            dma,
+            dma,
+            dma,
+            dma((4,)),
+            dma((2, 3)),
+            dma((2, 3)),
         ],
         compiler_params=pltpu.CompilerParams(
             collective_id=0, has_side_effects=True, vmem_limit_bytes=60 * 1024 * 1024
         ),
-    )(rows(spectrum_real), rows(spectrum_imag), *(jnp.asarray(t) for t in tables))
-
-
-def on_device(s, spectrum_real, spectrum_imag, volume, weights):
-    tv_grad = tv_gradient(volume, weights)
-    data = data_term(s, spectrum_real, spectrum_imag)
-    return volume - step_size * (data + tv_weight * tv_grad)
+    )(rows(spectrum_real), rows(spectrum_imag), *tables, volume, weights)
 
 
 def build(mesh, x_chips, shape):

time: 225 us -> 152 us (0.68)
  other arithmetic: 33.5 us -> 0 us
  starting transfers between devices: 16.2 us -> 0 us
  local copies, waits for them, and re-layouts: 14.2 us -> 3.16 us
  waiting for transfers between devices: 9.62 us -> 0 us
    ppermute x6 -> x0, starting transfers between devices: 16.2 us -> none  [the longest x3 11.3 us: padded_2(): before = lax.ppermute(last, axis, up)]
    mul x2 -> x0, other arithmetic: 9.65 us -> none  [the longest x1 6.27 us: tv_gradient(): flux_y = scaled * slope_y]
    ppermute x6 -> x0, waiting for transfers between devices: 9.62 us -> none  [the longest x3 7.85 us: padded_2(): after = lax.ppermute(initial, axis, down)]
    another operation x1 -> x0, other arithmetic: 7.82 us -> none  [tv_gradient(): stacked = jnp.stack([volume, weights])]
    concatenate x1 -> x0, other arithmetic: 7.33 us -> none  [padded_2(): x = jnp.concatenate([before, x, after], axis=dim)]
    sub x1 -> x0, other arithmetic: 6.5 us -> none  [on_device(): return volume - step_size * (data + tv_weight * tv_grad)]
    slice x2 -> x0, local copies, waits for them, and re-layouts: 5.92 us -> none  [the longest x1 2.96 us: padded_2(): initial = lax.slice_in_dim(x, 0, width, axis=dim)]
    ppermute x2 -> x0, local copies, waits for them, and re-layouts: 5.47 us -> none  [the longest x1 2.77 us: padded_2(): before = lax.ppermute(last, axis, up)]
  transfers between devices with their start and end apart: 6 -> 0, of which waited for: 3 -> 0; matrix products, arithmetic and copies ran while one was open for 3% -> 0% of each run, Pallas kernels for 67% -> 0%
where the time goes in v2:
time: 152 us
  Pallas kernels  149 us (98%)
  local copies, waits for them, and re-layouts  3.16 us (2%)
    pallas_call x1, Pallas kernels, on_device(): pl.pallas_call(functools.partial(kernel, s), out_shape=jax.ShapeDtypeStru...  149 us
    unnamed x1, local copies, waits for them, and re-layouts  3.16 us

profile of v2, /device:TPU:1, one launch (start us, length us, event | category | flops | bytes accessed | tf_op | source)
XLA Modules:
  0.0 151.9 jit_solution(12120111871075985421)
XLA Ops:
  0.0 148.8 %shard_map.73 = f32[64,64,128]{2,1,0:T(8,128)} custom-call(f32[4096,128]{1,0:T(8,128)} %bitcast.10, f32[4096,128]{1,0:T(8,128)} %bitcast.11, bf16[2,1024,512]{2,1,0:T(8,128)(2,1)} %constant.6.clone.tx, bf16[2,512,1024]{2,1,0:T(8,128)(2,1)} %constant.7.clone.ty_hbm, bf16[2,512,1024]{2,1,0:T(8,128)(2,1)} %constant.8.clone.tz_hbm, f32[64,64,128]{2,1,0:T(8,128)} %volume_hbm.1, ...), custom_call_target="tpu_custom_call" | custom-call | tf_op jit(solution)/shard_map/pallas_call | solution.py:414
  148.8 3.2 %copy.11 = f32[64,64,128]{2,1,0:T(8,128)} copy(f32[64,64,128]{2,1,0:T(8,128)} %shard_map.73) | data formatting | bytes 4194304

commit v3 on v2

v3 whole, which is shorter than its diff:
```python
import functools
import math

import jax
import jax.numpy as jnp
import ml_dtypes
import numpy as np
from jax import lax
from jax.experimental import pallas as pl
from jax.experimental.pallas import tpu as pltpu
from jax.sharding import PartitionSpec as P

step_size = 0.5
tv_weight = 0.5
smoothing = 0.5
MESH = pl.DeviceIdType.MESH
X_CHIPS = 4
CLASSES = 4


def halves(table):
    high = table.astype(ml_dtypes.bfloat16)
    low = (table - high.astype(np.float64)).astype(ml_dtypes.bfloat16)
    return np.stack([high, low])


def cos_sin(length, rows, columns):
    phases = (np.asarray(rows)[:, None] * np.asarray(columns)[None, :]) % length
    angles = phases * (2.0 * math.pi / length)
    factor = 1.0 / math.sqrt(length)
    return np.cos(angles) * factor, np.sin(angles) * factor


class Sizes:
    def __init__(self, mesh_sizes, x_chips, ny, nz, nx):
        self.gx, self.gy, self.gz = mesh_sizes
        self.ny, self.nz, self.nx = ny, nz, nx
        self.plane = self.gx * self.gy
        self.planes = nz // (self.plane * self.gz)
        self.chips = x_chips
        self.ring = self.plane // x_chips
        self.by, self.bz, self.bx = ny // self.gy, nz // self.gz, nx // self.gx
        self.classes = CLASSES
        self.class_y = ny // self.classes
        self.rows = self.by // (self.gz * self.classes)
        self.lines = 2 * nz


def make_tables(s):
    c, n = cos_sin(s.nx, range(s.nx), range(s.nx))
    table_x = halves(np.concatenate([c, n], axis=0))
    table_y = []
    for r in range(s.classes):
        c, n = cos_sin(s.ny, range(r, s.ny, s.classes), range(s.class_y))
        table_y.append(halves(np.concatenate([c, n], axis=1)))
    table_y = np.stack(table_y)
    r, g, k, x = np.meshgrid(
        range(s.ring), range(s.gz), range(s.planes), range(s.chips), indexing="ij"
    )
    kz = (((r * s.chips + x) * s.gz + g) * s.planes + k).reshape(-1)
    c, n = cos_sin(s.nz, range(s.nz), kz)
    table_z = halves(np.stack([c, -n], axis=-1).reshape(s.nz, s.lines))
    return table_x, table_y, table_z


def class_of(r, re, im):
    r = jnp.asarray(r, jnp.int32)
    if len(re) == 2:
        sign = (1 - 2 * r).astype(jnp.float32)
        return re[0] + sign * re[1], im[0] + sign * im[1]
    odd = r % 2
    pair = (1 - 2 * odd).astype(jnp.float32)
    sign = (1 - 2 * (r // 2)).astype(jnp.float32)
    even_sign, odd_sign = sign * (1 - odd).astype(jnp.float32), sign * odd.astype(jnp.float32)
    re_1, im_1 = re[1] + pair * re[3], im[1] + pair * im[3]
    re_0, im_0 = re[0] + pair * re[2], im[0] + pair * im[2]
    return re_0 + even_sign * re_1 - odd_sign * im_1, im_0 + even_sign * im_1 + odd_sign * re_1


def split(x):
    high = x.astype(jnp.bfloat16)
    return high, (x - high.astype(jnp.float32)).astype(jnp.bfloat16)


def dot3(a_high, a_low, b_high, b_low):
    f32 = jnp.float32
    return (
        jnp.dot(a_high, b_high, preferred_element_type=f32)
        + jnp.dot(a_high, b_low, preferred_element_type=f32)
        + jnp.dot(a_low, b_high, preferred_element_type=f32)
    )


def kernel(
    s, sr_hbm, si_hbm, tx_hbm, ty_hbm, tz_hbm, volume_hbm, weights_hbm, out,
    sr, si, tx, ty, tz, volume, weights,
    mine, blocks, pencils, lines, bricks, faces, halos,
    send1, recv1, send2, recv2, send3, recv3, load, face_send, face_recv,
):
    load_sr, load_si, load_ty, load_tx, load_volume, load_weights, load_tz = copies = [
        pltpu.make_async_copy(source, to, load.at[i])
        for i, (source, to) in enumerate(
            (
                (sr_hbm, sr),
                (si_hbm, si),
                (ty_hbm, ty),
                (tx_hbm, tx),
                (volume_hbm, volume.at[pl.ds(0, s.by)]),
                (weights_hbm, weights),
                (tz_hbm, tz),
            )
        )
    ]
    for copy in copies:
        copy.start()
    gx, gy, gz = lax.axis_index("gx"), lax.axis_index("gy"), lax.axis_index("gz")
    here = gx * s.gy + gy
    ring, chip = here // s.chips, here % s.chips
    lanes = s.nx // 128
    class_y = s.class_y

    def place(index):
        return (index // s.gy, index % s.gy, gz)

    def beside(step):
        return (gx, gy, (gz + step) % s.gz)

    barrier = pltpu.get_barrier_semaphore()

    def greet(i, _):
        pl.semaphore_signal(barrier, inc=1, device_id=place((here + i) % s.plane), device_id_type=MESH)
        return 0

    def greet_beside(i, _):
        pl.semaphore_signal(barrier, inc=1, device_id=beside(i), device_id_type=MESH)
        return 0

    lax.fori_loop(1, s.plane, greet, 0)
    lax.fori_loop(1, s.gz, greet_beside, 0)

    def transform(r, k):
        def quarters(ref):
            return [
                jnp.concatenate(
                    [
                        ref[q, pl.ds(k + j * s.planes, class_y, stride=lanes * s.planes), :]
                        for j in range(lanes)
                    ],
                    axis=1,
                )
                for q in range(s.classes)
            ]

        re, im = class_of(r, quarters(sr), quarters(si))
        re_high, re_low = split(re)
        im_high, im_low = split(im)
        y_high, y_low = ty[r, 0], ty[r, 1]
        real = dot3(
            y_high, y_low, jnp.concatenate([re_high, -im_high]), jnp.concatenate([re_low, -im_low])
        )
        imag = dot3(
            y_high, y_low, jnp.concatenate([im_high, re_high]), jnp.concatenate([im_low, re_low])
        )
        re_high, re_low = split(real)
        im_high, im_low = split(imag)
        high = jnp.concatenate(
            [jnp.concatenate([re_high, -im_high], 1), jnp.concatenate([im_high, re_high], 1)], 0
        )
        low = jnp.concatenate(
            [jnp.concatenate([re_low, -im_low], 1), jnp.concatenate([im_low, re_low], 1)], 0
        )
        both = dot3(high, low, tx[0], tx[1])
        for c in range(2):
            for q in range(s.gx):
                mine[r, q * s.gy : (q + 1) * s.gy, k, c] = both[
                    c * class_y : (c + 1) * class_y, q * 128 : (q + 1) * 128
                ].reshape(s.gy, s.gz, s.rows, 128)

    turns = []
    for h in range(1, s.ring // 2 + 1):
        turns += [h] if 2 * h == s.ring else [h, s.ring - h]

    def send_block(r, planes, turn, dx):
        to = ((ring + turn) % s.ring) * s.chips + (chip + dx) % s.chips
        pltpu.make_async_remote_copy(
            src_ref=mine.at[r, to, planes],
            dst_ref=blocks.at[r, planes, pl.ds(2 * here, 2)],
            send_sem=send1,
            recv_sem=recv1.at[r, ring],
            device_id=place(to),
            device_id_type=MESH,
        ).start()

    def send_class(r, first, planes):
        planes = pl.ds(first, planes)
        for turn in turns:
            lax.fori_loop(0, s.chips, lambda dx, _: (send_block(r, planes, turn, dx), 0)[1], 0)
        lax.fori_loop(1, s.chips, lambda dx, _: (send_block(r, planes, 0, dx), 0)[1], 0)
        pltpu.make_async_copy(
            mine.at[r, here, planes], blocks.at[r, planes, pl.ds(2 * here, 2)], recv1.at[r, ring]
        ).start()

    before_x, after_x = (gx + s.gx - 1) % s.gx, (gx + 1) % s.gx
    before_y, after_y = (gy + s.gy - 1) % s.gy, (gy + 1) % s.gy
    lane = lax.broadcasted_iota(jnp.int32, (s.bz, 128), 1)
    row = lax.broadcasted_iota(jnp.int32, (s.bz, 128), 0)
    unroll = 4

    def face_copies(stage, to_x, to_y, to_z):
        return [
            pltpu.make_async_remote_copy(
                src_ref=faces.at[stage, i],
                dst_ref=halos.at[stage, i],
                send_sem=face_send.at[stage, i],
                recv_sem=face_recv.at[stage, i],
                device_id=to,
                device_id_type=MESH,
            )
            for i, to in enumerate(((to_x, gy, gz), (gx, to_y, gz), (gx, gy, to_z)))
        ]

    volume_faces = face_copies(0, before_x, before_y, (gz + s.gz - 1) % s.gz)
    flux_faces = face_copies(1, after_x, after_y, (gz + 1) % s.gz)

    def send_faces():
        def step(i, face):
            for j in range(unroll):
                y = i * unroll + j
                face = jnp.where(lane == y, pltpu.roll(volume[y], y, 1), face)
            return face

        faces[0, 0, : s.bz] = lax.fori_loop(
            0, s.by // unroll, step, jnp.zeros((s.bz, 128), jnp.float32)
        )
        faces[0, 1, : s.bz] = volume[0]
        faces[0, 2, : s.by] = volume[: s.by, 0, :]
        for copy in volume_faces:
            copy.start()

    def fluxes_inside():
        for copy in volume_faces:
            copy.wait()
        volume[s.by] = jnp.where(gy == s.gy - 1, volume[s.by - 1], halos[0, 1, : s.bz])
        last_z = (row == s.bz - 1) & (gz == s.gz - 1)
        last_x = (lane == 127) & (gx == s.gx - 1)
        scale = step_size * tv_weight

        def one(y, before, face):
            v = volume[y]
            ahead_z = jnp.where(
                row == s.bz - 1, halos[0, 2, pl.ds(y, 1), :], pltpu.roll(v, s.bz - 1, 0)
            )
            ahead_x = jnp.where(
                lane == 127, pltpu.roll(halos[0, 0, : s.bz], 127 - y, 1), pltpu.roll(v, 127, 1)
            )
            slope_y = volume[y + 1] - v
            slope_z = jnp.where(last_z, 0.0, ahead_z - v)
            slope_x = jnp.where(last_x, 0.0, ahead_x - v)
            squares = slope_y * slope_y + slope_z * slope_z + slope_x * slope_x + smoothing
            scaled = weights[y] * lax.rsqrt(squares)
            flux_y, flux_z, flux_x = scaled * slope_y, scaled * slope_z, scaled * slope_x
            gradient = before - flux_y
            gradient = gradient + jnp.where(row == 0, 0.0, pltpu.roll(flux_z, 1, 0)) - flux_z
            gradient = gradient + jnp.where(lane == 0, 0.0, pltpu.roll(flux_x, 1, 1)) - flux_x
            faces[1, 2, pl.ds(y, 1), :] = flux_z[s.bz - 1 :]
            out[y] = v - scale * gradient
            return flux_y, jnp.where(lane == y, pltpu.roll(flux_x, y + 1, 1), face)

        def step(i, carry):
            for j in range(unroll):
                carry = one(i * unroll + j, *carry)
            return carry

        zero = jnp.zeros((s.bz, 128), jnp.float32)
        flux_y, face = lax.fori_loop(0, s.by // unroll, step, (zero, zero))
        faces[1, 0, : s.bz] = face
        faces[1, 1, : s.bz] = flux_y
        for copy in flux_faces:
            copy.start()

    def take_fluxes():
        scale = step_size * tv_weight
        for copy in flux_faces:
            copy.wait()
        out[0] = out[0] - jnp.where(gy == 0, 0.0, scale) * halos[1, 1, : s.bz]

    def first_classes(k, _):
        @pl.when(k == 0)
        def _():
            for copy in (load_sr, load_si, load_ty, load_tx):
                copy.wait()

        transform(0, k)

        @pl.when(k == 0)
        def _():
            pl.semaphore_wait(barrier, s.plane - 1 + s.gz - 1)

        send_class(0, k, 1)

        @pl.when(k == 0)
        def _():
            load_volume.wait()
            send_faces()

        return 0

    def transform_class(r):
        lax.fori_loop(0, s.planes, lambda k, _: (transform(r, k), 0)[1], 0)

    lax.fori_loop(0, s.planes, first_classes, 0)
    for later in range(1, s.classes):
        transform_class(later)
        send_class(later, 0, s.planes)

    width = 2 * s.chips

    def forward(r):
        for position, turn in enumerate(turns + [0]):
            source = (ring + s.ring - turn) % s.ring
            group = blocks.at[r, :, pl.ds(source * width, width)]
            pltpu.make_async_copy(group, group, recv1.at[r, source]).wait()

            def step(i, _):
                pltpu.make_async_remote_copy(
                    src_ref=blocks.at[r, :, pl.ds(source * width, width), (gz + i) % s.gz],
                    dst_ref=pencils.at[r, source, gz],
                    send_sem=send2,
                    recv_sem=recv2.at[r],
                    device_id=beside(i),
                    device_id_type=MESH,
                ).start()
                return 0

            lax.fori_loop(1, s.gz, step, 0)
            pltpu.make_async_copy(
                blocks.at[r, :, pl.ds(source * width, width), gz],
                pencils.at[r, source, gz],
                recv2.at[r],
            ).start()

    tile_z = min(256, s.nz)

    def transform_z(r, first):
        pieces = [
            split(pencils[r, :, :, :, :, first + j, :].reshape(s.lines, 128)) for j in range(2)
        ]
        high = jnp.concatenate([p[0] for p in pieces], axis=1)
        low = jnp.concatenate([p[1] for p in pieces], axis=1)
        for t in range(s.nz // tile_z):
            at = slice(t * tile_z, (t + 1) * tile_z)
            o = dot3(tz[0, at, :], tz[1, at, :], high, low)
            for j in range(2):
                lines[r, first + j, at, :] = o[:, j * 128 : (j + 1) * 128]

        def step(i, _):
            to = (gz + i) % s.gz
            pltpu.make_async_remote_copy(
                src_ref=lines.at[r, pl.ds(first, 2), pl.ds(to * s.bz, s.bz), :],
                dst_ref=bricks.at[r, gz, pl.ds(first, 2)],
                send_sem=send3,
                recv_sem=recv3.at[r],
                device_id=beside(i),
                device_id_type=MESH,
            ).start()
            return 0

        lax.fori_loop(1, s.gz, step, 0)
        pltpu.make_async_copy(
            lines.at[r, pl.ds(first, 2), pl.ds(gz * s.bz, s.bz), :],
            bricks.at[r, gz, pl.ds(first, 2)],
            recv3.at[r],
        ).start()

    def finish_class(r):
        pltpu.make_async_copy(bricks.at[r], bricks.at[r], recv3.at[r]).wait()

        def one_row(m, _):
            y = m * s.classes + r
            x_flux = pltpu.roll(halos[1, 0, : s.bz], (128 - y) % 128, 1)
            outer = jnp.where((lane == 0) & (gx > 0), x_flux, 0.0) + jnp.where(
                (row == 0) & (gz > 0), halos[1, 2, pl.ds(y, 1), :], 0.0
            )
            data = bricks[r, m // s.rows, m % s.rows]
            out[y] = out[y] - step_size * (data + tv_weight * outer)
            return 0

        lax.fori_loop(0, s.gz * s.rows, one_row, 0)

    def gather_class(r, _):
        forward(r)

        @pl.when(r == 0)
        def _():
            load_tz.wait()

        pltpu.make_async_copy(pencils.at[r], pencils.at[r], recv2.at[r]).wait()
        for first in range(0, s.rows, 2):
            transform_z(r, first)

        @pl.when(r == 0)
        def _():
            load_weights.wait()
            fluxes_inside()

        return 0

    lax.fori_loop(0, s.classes, gather_class, 0)
    take_fluxes()
    lax.fori_loop(0, s.classes, lambda r, _: (finish_class(r), 0)[1], 0)

    sent = mine.at[:, pl.ds(0, s.plane - 1)]
    pltpu.make_async_copy(sent, sent, send1).wait()
    sent = pencils.at[:, :, pl.ds(0, s.gz - 1)]
    pltpu.make_async_copy(sent, sent, send2).wait()
    sent = bricks.at[:, pl.ds(0, s.gz - 1)]
    pltpu.make_async_copy(sent, sent, send3).wait()


def on_device(s, spectrum_real, spectrum_imag, volume, weights):
    tables = [jnp.asarray(t) for t in make_tables(s)]

    def rows(x):
        x = x.reshape(s.ny, s.planes, s.nx // 128, 128)
        return x.transpose(0, 2, 1, 3).reshape(s.classes, -1, 128)

    f32, bf16 = jnp.float32, jnp.bfloat16
    brick = (s.by, s.bz, s.bx)
    spectrum = (s.classes, s.class_y * s.planes * s.nx // 128, 128)
    face = max(s.by, s.bz)
    dma = pltpu.SemaphoreType.DMA
    return pl.pallas_call(
        functools.partial(kernel, s),
        out_shape=jax.ShapeDtypeStruct(brick, f32),
        in_specs=[pl.BlockSpec(memory_space=pl.ANY)] * 7,
        out_specs=pl.BlockSpec(memory_space=pltpu.VMEM),
        scratch_shapes=[
            pltpu.VMEM(spectrum, f32),
            pltpu.VMEM(spectrum, f32),
            *(pltpu.VMEM(table.shape, bf16) for table in tables),
            pltpu.VMEM((s.by + 1, s.bz, s.bx), f32),
            pltpu.VMEM(brick, f32),
            pltpu.VMEM((s.classes, s.plane, s.planes, 2, s.gz, s.rows, 128), f32),
            pltpu.VMEM((s.classes, s.planes, 2 * s.plane, s.gz, s.rows, 128), f32),
            pltpu.VMEM((s.classes, s.ring, s.gz, s.planes, 2 * s.chips, s.rows, 128), f32),
            pltpu.VMEM((s.classes, s.rows, s.nz, 128), f32),
            pltpu.VMEM((s.classes, s.gz, s.rows, s.bz, 128), f32),
            pltpu.VMEM((2, 3, face, 128), f32),
            pltpu.VMEM((2, 3, face, 128), f32),
            dma,
            dma((s.classes, s.ring)),
            dma,
            dma((s.classes,)),
            dma,
            dma((s.classes,)),
            dma((7,)),
            dma((2, 3)),
            dma((2, 3)),
        ],
        compiler_params=pltpu.CompilerParams(
            collective_id=0, has_side_effects=True, vmem_limit_bytes=62 * 1024 * 1024
        ),
    )(rows(spectrum_real), rows(spectrum_imag), *tables, volume, weights)


def build(mesh, x_chips, shape):
    sizes = Sizes([mesh.shape[a] for a in ("gx", "gy", "gz")], x_chips, *shape)
    spectrum, brick = P(None, ("gx", "gy", "gz"), None), P("gy", "gz", "gx")
    return jax.shard_map(
        functools.partial(on_device, sizes),
        mesh=mesh,
        in_specs=(spectrum, spectrum, brick, brick),
        out_specs=brick,
        check_vma=False,
    )


def solution(mesh):
    return build(mesh, X_CHIPS, (512, 512, 512))
```

time: 152 us -> 131 us (0.86)
  Pallas kernels: 149 us -> 128 us
    pallas_call x1, Pallas kernels: 149 us -> 128 us  [on_device(): pl.pallas_call(functools.partial(kernel, s), out_shape=jax.ShapeDtypeStru...]
where the time goes in v3:
time: 131 us
  Pallas kernels  128 us (98%)
  local copies, waits for them, and re-layouts  3.16 us (2%)
    pallas_call x1, Pallas kernels, on_device(): pl.pallas_call(functools.partial(kernel, s), out_shape=jax.ShapeDtypeStru...  128 us
    unnamed x1, local copies, waits for them, and re-layouts  3.16 us

profile of v3, /device:TPU:1, one launch (start us, length us, event | category | flops | bytes accessed | tf_op | source)
XLA Modules:
  0.0 131.2 jit_solution(15052459160438778500)
XLA Ops:
  0.0 128.0 %shard_map.73 = f32[64,64,128]{2,1,0:T(8,128)} custom-call(f32[4,1024,128]{2,1,0:T(8,128)} %bitcast.10, f32[4,1024,128]{2,1,0:T(8,128)} %bitcast.11, bf16[2,1024,512]{2,1,0:T(8,128)(2,1)} %constant.6.clone.tx_hbm, bf16[4,2,128,256]{3,2,1,0:T(8,128)(2,1)} %constant.7.clone.ty_hbm, bf16[2,512,1024]{2,1,0:T(8,128)(2,1)} %constant.8.clone.tz_hbm, ...), custom_call_target="tpu_custom_call" | custom-call | tf_op jit(solution)/shard_map/pallas_call | solution.py:432
  128.0 3.2 %copy.11 = f32[64,64,128]{2,1,0:T(8,128)} copy(f32[64,64,128]{2,1,0:T(8,128)} %shard_map.73) | data formatting | bytes 4194304

commit v4 on v3

--- a/solution.py
+++ b/solution.py
@@ -16,6 +16,7 @@
 MESH = pl.DeviceIdType.MESH
 X_CHIPS = 4
 CLASSES = 4
+DELIVERIES = 8
 
 
 def halves(table):
@@ -92,10 +93,10 @@
 
 
 def kernel(
-    s, sr_hbm, si_hbm, tx_hbm, ty_hbm, tz_hbm, volume_hbm, weights_hbm, out,
+    s, sr_hbm, si_hbm, tx_hbm, ty_hbm, tz_hbm, volume_hbm, weights_hbm, result,
     sr, si, tx, ty, tz, volume, weights,
-    mine, blocks, pencils, lines, bricks, faces, halos,
-    send1, recv1, send2, recv2, send3, recv3, load, face_send, face_recv,
+    out, mine, blocks, pencils, lines, bricks, faces, halos,
+    send1, recv1, send2, recv2, send3, recv3, load, store, face_send, face_recv,
 ):
     load_sr, load_si, load_ty, load_tx, load_volume, load_weights, load_tz = copies = [
         pltpu.make_async_copy(source, to, load.at[i])
@@ -111,7 +112,7 @@
             )
         )
     ]
-    for copy in copies:
+    for copy in copies[:4]:
         copy.start()
     gx, gy, gz = lax.axis_index("gx"), lax.axis_index("gy"), lax.axis_index("gz")
     here = gx * s.gy + gy
@@ -263,7 +264,7 @@
             gradient = gradient + jnp.where(row == 0, 0.0, pltpu.roll(flux_z, 1, 0)) - flux_z
             gradient = gradient + jnp.where(lane == 0, 0.0, pltpu.roll(flux_x, 1, 1)) - flux_x
             faces[1, 2, pl.ds(y, 1), :] = flux_z[s.bz - 1 :]
-            out[y] = v - scale * gradient
+            out[y // s.classes, y % s.classes] = v - scale * gradient
             return flux_y, jnp.where(lane == y, pltpu.roll(flux_x, y + 1, 1), face)
 
         def step(i, carry):
@@ -282,7 +283,7 @@
         scale = step_size * tv_weight
         for copy in flux_faces:
             copy.wait()
-        out[0] = out[0] - jnp.where(gy == 0, 0.0, scale) * halos[1, 1, : s.bz]
+        out[0, 0] = out[0, 0] - jnp.where(gy == 0, 0.0, scale) * halos[1, 1, : s.bz]
 
     def first_classes(k, _):
         @pl.when(k == 0)
@@ -300,6 +301,8 @@
 
         @pl.when(k == 0)
         def _():
+            for copy in copies[4:]:
+                copy.start()
             load_volume.wait()
             send_faces()
 
@@ -372,20 +375,26 @@
             recv3.at[r],
         ).start()
 
+    def store_class(r):
+        return pltpu.make_async_copy(out.at[:, r], result.at[:, r], store.at[r])
+
     def finish_class(r):
         pltpu.make_async_copy(bricks.at[r], bricks.at[r], recv3.at[r]).wait()
 
-        def one_row(m, _):
-            y = m * s.classes + r
-            x_flux = pltpu.roll(halos[1, 0, : s.bz], (128 - y) % 128, 1)
-            outer = jnp.where((lane == 0) & (gx > 0), x_flux, 0.0) + jnp.where(
-                (row == 0) & (gz > 0), halos[1, 2, pl.ds(y, 1), :], 0.0
-            )
-            data = bricks[r, m // s.rows, m % s.rows]
-            out[y] = out[y] - step_size * (data + tv_weight * outer)
+        def some_rows(i, _):
+            for j in range(unroll):
+                m = i * unroll + j
+                y = m * s.classes + r
+                x_flux = pltpu.roll(halos[1, 0, : s.bz], (128 - y) % 128, 1)
+                outer = jnp.where((lane == 0) & (gx > 0), x_flux, 0.0) + jnp.where(
+                    (row == 0) & (gz > 0), halos[1, 2, pl.ds(y, 1), :], 0.0
+                )
+                data = bricks[r, m // s.rows, m % s.rows]
+                out[m, r] = out[m, r] - step_size * (data + tv_weight * outer)
             return 0
 
-        lax.fori_loop(0, s.gz * s.rows, one_row, 0)
+        lax.fori_loop(0, s.gz * s.rows // unroll, some_rows, 0)
+        store_class(r).start()
 
     def gather_class(r, _):
         forward(r)
@@ -403,11 +412,18 @@
             load_weights.wait()
             fluxes_inside()
 
+        @pl.when(r == s.classes - 1)
+        def _():
+            take_fluxes()
+            for ready in range(s.classes - 1):
+                finish_class(ready)
+
         return 0
 
     lax.fori_loop(0, s.classes, gather_class, 0)
-    take_fluxes()
-    lax.fori_loop(0, s.classes, lambda r, _: (finish_class(r), 0)[1], 0)
+    finish_class(s.classes - 1)
+    for ready in range(s.classes):
+        store_class(ready).wait()
 
     sent = mine.at[:, pl.ds(0, s.plane - 1)]
     pltpu.make_async_copy(sent, sent, send1).wait()
@@ -417,6 +433,40 @@
     pltpu.make_async_copy(sent, sent, send3).wait()
 
 
+def deliver_kernel(source, to, held, taken, done):
+    rows = source.shape[0] // DELIVERIES
+    parts = [pl.ds(i * rows, rows) for i in range(DELIVERIES)]
+    take = [
+        pltpu.make_async_copy(source.at[part], held.at[part], taken.at[i])
+        for i, part in enumerate(parts)
+    ]
+    give = [
+        pltpu.make_async_copy(held.at[part], to.at[part], done.at[i])
+        for i, part in enumerate(parts)
+    ]
+    for copy in take:
+        copy.start()
+    for first, second in zip(take, give):
+        first.wait()
+        second.start()
+    for copy in give:
+        copy.wait()
+
+
+def deliver(x):
+    return pl.pallas_call(
+        deliver_kernel,
+        out_shape=jax.ShapeDtypeStruct(x.shape, x.dtype),
+        in_specs=[pl.BlockSpec(memory_space=pl.ANY)],
+        out_specs=pl.BlockSpec(memory_space=pl.ANY),
+        scratch_shapes=[
+            pltpu.VMEM(x.shape, x.dtype),
+            pltpu.SemaphoreType.DMA((DELIVERIES,)),
+            pltpu.SemaphoreType.DMA((DELIVERIES,)),
+        ],
+    )(x)
+
+
 def on_device(s, spectrum_real, spectrum_imag, volume, weights):
     tables = [jnp.asarray(t) for t in make_tables(s)]
 
@@ -426,20 +476,22 @@
 
     f32, bf16 = jnp.float32, jnp.bfloat16
     brick = (s.by, s.bz, s.bx)
+    classed = (s.by // s.classes, s.classes, s.bz, s.bx)
     spectrum = (s.classes, s.class_y * s.planes * s.nx // 128, 128)
     face = max(s.by, s.bz)
     dma = pltpu.SemaphoreType.DMA
-    return pl.pallas_call(
+    updated = pl.pallas_call(
         functools.partial(kernel, s),
-        out_shape=jax.ShapeDtypeStruct(brick, f32),
+        out_shape=jax.ShapeDtypeStruct(classed, f32),
         in_specs=[pl.BlockSpec(memory_space=pl.ANY)] * 7,
-        out_specs=pl.BlockSpec(memory_space=pltpu.VMEM),
+        out_specs=pl.BlockSpec(memory_space=pl.ANY),
         scratch_shapes=[
             pltpu.VMEM(spectrum, f32),
             pltpu.VMEM(spectrum, f32),
             *(pltpu.VMEM(table.shape, bf16) for table in tables),
             pltpu.VMEM((s.by + 1, s.bz, s.bx), f32),
             pltpu.VMEM(brick, f32),
+            pltpu.VMEM(classed, f32),
             pltpu.VMEM((s.classes, s.plane, s.planes, 2, s.gz, s.rows, 128), f32),
             pltpu.VMEM((s.classes, s.planes, 2 * s.plane, s.gz, s.rows, 128), f32),
             pltpu.VMEM((s.classes, s.ring, s.gz, s.planes, 2 * s.chips, s.rows, 128), f32),
@@ -454,6 +506,7 @@
             dma,
             dma((s.classes,)),
             dma((7,)),
+            dma((s.classes,)),
             dma((2, 3)),
             dma((2, 3)),
         ],
@@ -461,6 +514,7 @@
             collective_id=0, has_side_effects=True, vmem_limit_bytes=62 * 1024 * 1024
         ),
     )(rows(spectrum_real), rows(spectrum_imag), *tables, volume, weights)
+    return deliver(updated.reshape(brick))
 
 
 def build(mesh, x_chips, shape):

time: 131 us -> 129 us (0.985)
  local copies, waits for them, and re-layouts: 3.16 us -> 0 us
    unnamed x1 -> x0, local copies, waits for them, and re-layouts: 3.16 us -> none
    pallas_call x0 -> x1, Pallas kernels: none -> 2.39 us  [deliver(): pl.pallas_call(deliver_kernel, out_shape=jax.ShapeDtypeStruct(x.shape, x....]
    pallas_call x1, Pallas kernels: 128 us -> 126 us  [on_device(): pl.pallas_call(functools.partial(kernel, s), out_shape=jax.ShapeDtypeStru...]
where the time goes in v4:
time: 129 us
  Pallas kernels  129 us (100%)
    pallas_call x1, Pallas kernels, on_device(): pl.pallas_call(functools.partial(kernel, s), out_shape=jax.ShapeDtypeStru...  126 us

profile of v4, /device:TPU:1, one launch (start us, length us, event | category | flops | bytes accessed | tf_op | source)
XLA Modules:
  0.0 128.5 jit_solution(4467915323389008703)
XLA Ops:
  0.0 126.1 %shard_map.73 = f32[16,4,64,128]{3,2,1,0:T(8,128)} custom-call(f32[4,1024,128]{2,1,0:T(8,128)} %bitcast.12, f32[4,1024,128]{2,1,0:T(8,128)} %bitcast.13, bf16[2,1024,512]{2,1,0:T(8,128)(2,1)} %constant.6.clone.tx_hbm, bf16[4,2,128,256]{3,2,1,0:T(8,128)(2,1)} %constant.7.clone.ty_hbm, bf16[2,512,1024]{2,1,0:T(8,128)(2,1)} %constant.8.clone.tz_hbm, ...), custom_call_target="tpu_custom_call" | custom-call | tf_op jit(solution)/shard_map/pallas_call | solution.py:483
  126.1 2.4 %shard_map.74 = f32[64,64,128]{2,1,0:T(8,128)} custom-call(f32[64,64,128]{2,1,0:T(8,128)} %bitcast.11), custom_call_target="tpu_custom_call" | custom-call | tf_op jit(solution)/shard_map/pallas_call | solution.py:457

commit v5 on v4

--- a/solution.py
+++ b/solution.py
@@ -136,10 +136,12 @@
         pl.semaphore_signal(barrier, inc=1, device_id=beside(i), device_id_type=MESH)
         return 0
 
-    lax.fori_loop(1, s.plane, greet, 0)
-    lax.fori_loop(1, s.gz, greet_beside, 0)
-
-    def transform(r, k):
+    for i in range(1, s.plane):
+        greet(i, 0)
+    for i in range(1, s.gz):
+        greet_beside(i, 0)
+
+    def transform(r, k, before_x=None):
         def quarters(ref):
             return [
                 jnp.concatenate(
@@ -162,6 +164,8 @@
         imag = dot3(
             y_high, y_low, jnp.concatenate([im_high, re_high]), jnp.concatenate([im_low, re_low])
         )
+        if before_x is not None:
+            before_x()
         re_high, re_low = split(real)
         im_high, im_low = split(imag)
         high = jnp.concatenate(
@@ -288,10 +292,15 @@
     def first_classes(k, _):
         @pl.when(k == 0)
         def _():
-            for copy in (load_sr, load_si, load_ty, load_tx):
+            for copy in (load_sr, load_si, load_ty):
                 copy.wait()
 
-        transform(0, k)
+        def wait_tx():
+            @pl.when(k == 0)
+            def _():
+                load_tx.wait()
+
+        transform(0, k, wait_tx)
 
         @pl.when(k == 0)
         def _():
@@ -317,6 +326,7 @@
         send_class(later, 0, s.planes)
 
     width = 2 * s.chips
+    far_first = sorted(range(1, s.gz), key=lambda i: (-min(i, s.gz - i), i))
 
     def forward(r):
         for position, turn in enumerate(turns + [0]):
@@ -335,7 +345,8 @@
                 ).start()
                 return 0
 
-            lax.fori_loop(1, s.gz, step, 0)
+            for i in far_first:
+                step(i, 0)
             pltpu.make_async_copy(
                 blocks.at[r, :, pl.ds(source * width, width), gz],
                 pencils.at[r, source, gz],
@@ -368,7 +379,8 @@
             ).start()
             return 0
 
-        lax.fori_loop(1, s.gz, step, 0)
+        for i in far_first:
+            step(i, 0)
         pltpu.make_async_copy(
             lines.at[r, pl.ds(first, 2), pl.ds(gz * s.bz, s.bz), :],
             bricks.at[r, gz, pl.ds(first, 2)],

time: 129 us -> 127 us (0.984)
  Pallas kernels: 129 us -> 126 us
    pallas_call x1, Pallas kernels: 126 us -> 124 us  [on_device(): pl.pallas_call(functools.partial(kernel, s), out_shape=jax.ShapeDtypeStru...]
where the time goes in v5:
time: 127 us; the launch traced here: 126 us
  Pallas kernels  126 us (99%)
    pallas_call x1, Pallas kernels, on_device(): pl.pallas_call(functools.partial(kernel, s), out_shape=jax.ShapeDtypeStru...  124 us

profile of v5, /device:TPU:1, one launch (start us, length us, event | category | flops | bytes accessed | tf_op | source)
XLA Modules:
  0.0 126.4 jit_solution(1859431708518687587)
XLA Ops:
  0.0 124.0 %shard_map.73 = f32[16,4,64,128]{3,2,1,0:T(8,128)} custom-call(f32[4,1024,128]{2,1,0:T(8,128)} %bitcast.12, f32[4,1024,128]{2,1,0:T(8,128)} %bitcast.13, bf16[2,1024,512]{2,1,0:T(8,128)(2,1)} %constant.6.clone.tx_hbm, bf16[4,2,128,256]{3,2,1,0:T(8,128)(2,1)} %constant.7.clone.ty_hbm, bf16[2,512,1024]{2,1,0:T(8,128)(2,1)} %constant.8.clone.tz_hbm, ...), custom_call_target="tpu_custom_call" | custom-call | tf_op jit(solution)/shard_map/pallas_call | solution.py:495
  124.0 2.4 %shard_map.74 = f32[64,64,128]{2,1,0:T(8,128)} custom-call(f32[64,64,128]{2,1,0:T(8,128)} %bitcast.11), custom_call_target="tpu_custom_call" | custom-call | tf_op jit(solution)/shard_map/pallas_call | solution.py:469

commit v6 on v5

--- a/solution.py
+++ b/solution.py
@@ -185,6 +185,8 @@
     for h in range(1, s.ring // 2 + 1):
         turns += [h] if 2 * h == s.ring else [h, s.ring - h]
 
+    far_chips = sorted(range(1, s.chips), key=lambda i: (-min(i, s.chips - i), i))
+
     def send_block(r, planes, turn, dx):
         to = ((ring + turn) % s.ring) * s.chips + (chip + dx) % s.chips
         pltpu.make_async_remote_copy(
@@ -199,8 +201,10 @@
     def send_class(r, first, planes):
         planes = pl.ds(first, planes)
         for turn in turns:
-            lax.fori_loop(0, s.chips, lambda dx, _: (send_block(r, planes, turn, dx), 0)[1], 0)
-        lax.fori_loop(1, s.chips, lambda dx, _: (send_block(r, planes, 0, dx), 0)[1], 0)
+            for dx in far_chips + [0]:
+                send_block(r, planes, turn, dx)
+        for dx in far_chips:
+            send_block(r, planes, 0, dx)
         pltpu.make_async_copy(
             mine.at[r, here, planes], blocks.at[r, planes, pl.ds(2 * here, 2)], recv1.at[r, ring]
         ).start()

time: 127 us -> 126 us (level)
    pallas_call x1, Pallas kernels: 124 us -> 123 us  [on_device(): pl.pallas_call(functools.partial(kernel, s), out_shape=jax.ShapeDtypeStru...]
where the time goes in v6:
time: 126 us; the launch traced here: 125 us
  Pallas kernels  125 us (99%)
    pallas_call x1, Pallas kernels, on_device(): pl.pallas_call(functools.partial(kernel, s), out_shape=jax.ShapeDtypeStru...  123 us

profile of v6, /device:TPU:1, one launch (start us, length us, event | category | flops | bytes accessed | tf_op | source)
XLA Modules:
  0.0 125.0 jit_solution(1040398170629210569)
XLA Ops:
  0.0 122.6 %shard_map.73 = f32[16,4,64,128]{3,2,1,0:T(8,128)} custom-call(f32[4,1024,128]{2,1,0:T(8,128)} %bitcast.12, f32[4,1024,128]{2,1,0:T(8,128)} %bitcast.13, bf16[2,1024,512]{2,1,0:T(8,128)(2,1)} %constant.6.clone.tx_hbm, bf16[4,2,128,256]{3,2,1,0:T(8,128)(2,1)} %constant.7.clone.ty_hbm, bf16[2,512,1024]{2,1,0:T(8,128)(2,1)} %constant.8.clone.tz_hbm, ...), custom_call_target="tpu_custom_call" | custom-call | tf_op jit(solution)/shard_map/pallas_call | solution.py:499
  122.6 2.4 %shard_map.74 = f32[64,64,128]{2,1,0:T(8,128)} custom-call(f32[64,64,128]{2,1,0:T(8,128)} %bitcast.11), custom_call_target="tpu_custom_call" | custom-call | tf_op jit(solution)/shard_map/pallas_call | solution.py:473
